TPU v7x, 32 devices: a whole 2x2x4 slice. The times are simulated.
32 devices in a mesh: gx: 4 (over y, core), gy: 4 (over z), gz: 2 (over x).
Axes of the slice: x: 2, y: 2, z: 4, core: 2. Of those that a mesh axis runs over, the one named last changes fastest.
Arguments:
- positions: float32 [3, 4, 4, 2, 512], P(None, 'gx', 'gy', 'gz'), may hold values from -6 to 6
- velocity: float32 [3, 4, 4, 2, 512], P(None, 'gx', 'gy', 'gz'), may hold values from -7.2 to 7.2
- atom_eps: float32 [4, 4, 2, 512], P('gx', 'gy', 'gz'), may hold values from 0.5 to 2
- neighbours: int32 [4, 4, 2, 32, 512], P('gx', 'gy', 'gz'), may hold values from 0 to 511
- pair_live: int32 [4, 4, 2, 32, 512], P('gx', 'gy', 'gz'), may hold values 0 or 1
- event_count: int32 [4, 4, 2], P('gx', 'gy', 'gz'), may hold values from 0 to 16, as said below
- event_atoms: int32 [4, 4, 2, 16, 128], P('gx', 'gy', 'gz'), may hold values from 0 to 1023
- event_weight: float32 [4, 4, 2, 16], P('gx', 'gy', 'gz'), may hold values from 0.2 to 1
- template_map: float32 [128, 128], replicated, may hold values from -0.5 to 0.5
Outputs:
- final_positions: float32 [3, 4, 4, 2, 512], P(None, 'gx', 'gy', 'gz')
- final_velocity: float32 [3, 4, 4, 2, 512], P(None, 'gx', 'gy', 'gz')
Inputs may be any that keep to these rules, and one draw needn't show every extreme that they name: `event_count`: in every column of domains along the third dimension, the counts add up to at most 32, and one domain of the column holds 16.
All inputs are finite; a program needn't handle non-finite values. No bound on the sum of `pair_live` on one device may be relied on, other than what follows from the above.
Results may differ from a plain program's by a relative error of at most 0.0003.
Values sent between devices are 32-bit elements; how exact they have to be, the bound alone decides.
A program may use at most 64 MiB of HBM per device.

v0:
```python
import jax
import jax.numpy as jnp
from jax import lax
from jax.sharding import PartitionSpec as P

EV_DEV = 16
NEIGH = 32
TEMPLATE = 128
FIRE_STEPS = 2


width_scale = 1.5
time_step = 0.1
mixing = 0.1
epsilon = 1e-06


def with_halo(x, sides, width):
    for axis, dim in sides:
        size, length = (lax.axis_size(axis), x.shape[dim])
        up = [(i, (i + 1) % size) for i in range(size)]
        down = [(j, i) for i, j in up]
        last = lax.slice_in_dim(x, length - width, length, axis=dim)
        leading = lax.slice_in_dim(x, 0, width, axis=dim)
        before = lax.ppermute(last, axis, up)
        after = lax.ppermute(leading, axis, down)
        x = jnp.concatenate([before, x, after], axis=dim)
    return x


def relax_events(group_positions, members, weights, template_map):
    gathered = jnp.take(group_positions, members, axis=1)
    centred = gathered - jnp.mean(gathered, axis=2, keepdims=True)
    shifted = jnp.einsum("cnt,ts->cns", centred, template_map, precision=lax.Precision.HIGHEST)
    shifted = shifted * weights[None, :, None]
    flattened = members.reshape(-1)
    return jnp.zeros_like(group_positions).at[:, flattened].add(shifted.reshape(3, -1))


def pair_forces(neighbourhood, own_atoms, neighbour_rows, live_pairs):
    partner = jnp.take(neighbourhood, neighbour_rows, axis=1)
    separation = own_atoms[:3, None, :] - partner[:3]
    distance_sq = jnp.sum(separation * separation, axis=0)
    strength = jnp.sqrt(own_atoms[3][None, :] * partner[3]) * live_pairs.astype(jnp.float32)
    strength = (
        strength
        * jnp.exp(-distance_sq * (0.5 / (width_scale * width_scale)))
        / (width_scale * width_scale)
    )
    return jnp.sum(strength[None] * separation, axis=1)


def shards(
    positions,
    velocity,
    atom_eps,
    neighbours,
    pair_live,
    event_count,
    event_atoms,
    event_weight,
    template_map,
):
    atom_count = positions.shape[4]
    group_size = lax.axis_size("gz")
    gathered = lax.all_gather(positions, "gz", axis=3, tiled=True)
    group_positions = gathered.reshape(3, group_size * atom_count)
    alive_mask = jnp.arange(EV_DEV, dtype=jnp.int32) < event_count.reshape(())
    members = event_atoms.reshape(EV_DEV, TEMPLATE)
    weights = event_weight.reshape(EV_DEV) * alive_mask.astype(jnp.float32)
    displaced = relax_events(group_positions, members, weights, template_map).reshape(
        3, 1, 1, group_size, atom_count
    )
    returned = lax.psum_scatter(displaced, "gz", scatter_dimension=3, tiled=True)
    moved_positions = positions + returned
    offsets = jnp.arange(NEIGH, dtype=jnp.int32) % 27 * atom_count
    neighbour_rows = neighbours.reshape(NEIGH, atom_count) + offsets[:, None]
    live_pairs = pair_live.reshape(NEIGH, atom_count)
    speeds = velocity
    for iteration in range(FIRE_STEPS):
        packed = jnp.concatenate([moved_positions, atom_eps[None]], 0)
        widened = with_halo(packed, (("gx", 1), ("gy", 2), ("gz", 3)), 1)
        neighbourhood = widened.reshape(4, 27 * atom_count)
        forces = pair_forces(
            neighbourhood, packed.reshape(4, atom_count), neighbour_rows, live_pairs
        ).reshape(moved_positions.shape)
        power_sum, speed_sq, force_sq = lax.psum(
            (jnp.sum(forces * speeds), jnp.sum(speeds * speeds), jnp.sum(forces * forces)),
            ("gx", "gy", "gz"),
        )
        cosine = power_sum / (jnp.sqrt(speed_sq + epsilon) * jnp.sqrt(force_sq + epsilon))
        speed_ratio = jnp.sqrt((speed_sq + epsilon) / (force_sq + epsilon))
        speeds = 0.5 * (1.0 + cosine) * ((1.0 - mixing) * speeds + mixing * speed_ratio * forces)
        speeds = speeds + time_step * forces
        moved_positions = moved_positions + time_step * speeds
    return (moved_positions, speeds)


def solution(mesh):
    in_specs = (
        P(None, "gx", "gy", "gz", None),
        P(None, "gx", "gy", "gz", None),
        P("gx", "gy", "gz", None),
        P("gx", "gy", "gz", None, None),
        P("gx", "gy", "gz", None, None),
        P("gx", "gy", "gz"),
        P("gx", "gy", "gz", None, None),
        P("gx", "gy", "gz", None),
        P(),
    )
    out_specs = (P(None, "gx", "gy", "gz", None), P(None, "gx", "gy", "gz", None))
    return jax.shard_map(shards, mesh=mesh, in_specs=in_specs, out_specs=out_specs, check_vma=False)
```

profile of v0, /device:TPU:0, one launch (start us, length us, event | category | flops | bytes accessed | tf_op | source)
XLA Modules:
  0.0 295.9 jit_solution(7192560058389783281)
XLA Ops:
  0.6 0.0 copy-start
  0.7 0.7 compare_and_fusion.1
  1.4 0.7 fusion.47
  2.7 0.7 compare_select_fusion.1
  3.5 5.5 %all_gather.3 = f32[3,1,1,2,512]{4,2,1,0,3:T(1,128)S(1)} all-gather(f32[3,1,1,1,512]{4,2,1,0,3:T(1,128)} %bitcast.113), channel_id=1, replica_groups=mesh['gx'=4,'gy'=4,'gz'=2] {'gz'}, dimensions={3}, use_global_device_ids=true | all-gather | bytes 18432 | tf_op jit(solution)/shard_map/all_gather | solution.py:66
  9.0 0.2 copy.20
  9.2 5.5 %gather_fusion = f32[2048,3]{1,0:T(8,128)S(1)} fusion(f32[3,1024]{0,1:T(8,128)S(1)} %bitcast.96, s32[2048]{0:T(1024)S(1)} %fusion.47), kind=kCustom, calls=%fused_computation.2 | custom fusion | bytes 57344 | tf_op jit(solution)/shard_map/jit(_take)/gather | solution.py:32
  14.7 0.3 copy.21
  15.0 0.1 bitcast_reduce_fusion
  15.1 0.7 compare_select_fusion.4
  15.8 0.2 convolution_multiply_fusion
  16.0 0.4 copy.33
  16.4 11.6 %scatter_custom_fusion = f32[3,1024]{0,1:T(8,128)S(1)} fusion(s32[2048]{0:T(1024)S(1)} %bitcast.114, f32[2048,3]{1,0:T(8,128)S(1)} %bitcast.95, f32[]{:T(128)} %constant.20.clone.1), kind=kCustom, calls=%fused_computation.9 | custom fusion | flops 6144 | bytes 12292 | tf_op jit(solution)/shard_map/scatter-add | solution.py:37
  28.0 0.2 copy.23
  28.2 8.6 %all-reduce = f32[3,1,1,2,512]{4,0,2,1,3:T(4,128)S(1)} all-reduce(f32[3,1,1,2,512]{4,0,2,1,3:T(4,128)S(1)} %copy.23), channel_id=2, replica_groups=mesh['gx'=4,'gy'=4,'gz'=2] {'gz'}, use_global_device_ids=true, to_apply=%region_2.3.clone | all-reduce | flops 3072 | bytes 24576
  36.8 1.2 dynamic-slice
  38.1 1.3 dynamic-slice_add_fusion
  39.4 0.7 pad_maximum_fusion.7
  40.1 0.0 collective-permute-start.1
  40.1 0.5 collective-permute-start
  40.6 0.9 fusion.33
  41.6 1.7 collective-permute-done
  43.3 0.7 fusion.35
  44.0 3.7 %collective-permute-start.3 = (f32[4,3,1,1,512]{4,0,2,1,3:T(4,128)S(1)}, f32[4,3,1,1,512]{4,0,2,1,3:T(4,128)S(1)}, u32[]{:S(2)}, u32[]{:S(2)}) collective-permute-start(f32[4,3,1,1,512]{4,0,2,1,3:T(4,128)S(1)} %fusion.35), channel_id=1, source_target_pairs={{2,0},{4,2},{6,4},{0,6},{3,1},{5,3},{7,5},{1,7},{10,8},{12,10},{14... | collective-permute-start | bytes 73736 | tf_op jit(solution)/shard_map/ppermute | solution.py:26
  47.7 0.9 compare_and_fusion
  48.6 0.6 collective-permute-done.3
  49.2 4.1 %collective-permute-done.2 = f32[4,3,1,1,512]{4,0,2,1,3:T(4,128)S(1)} collective-permute-done((f32[4,3,1,1,512]{4,0,2,1,3:T(4,128)S(1)}, f32[4,3,1,1,512]{4,0,2,1,3:T(4,128)S(1)}, u32[]{:S(2)}, u32[]{:S(2)}) %collective-permute-start.2) | collective-permute-done | bytes 24608 | tf_op jit(solution)/shard_map/ppermute | solution.py:25
  53.3 0.7 fusion.17
  54.0 0.6 collective-permute-start.5
  54.6 1.5 collective-permute-start.4
  56.1 1.3 multiply_reduce_fusion.7
  57.4 1.0 collective-permute-done.5
  58.4 0.8 collective-permute-done.4
  59.2 0.7 fusion.7
  59.9 0.0 copy-start.1
  60.0 0.0 copy-start.2
  60.0 0.0 copy-start.3
  60.0 4.3 %copy.25 = f32[4,3,3,3,512]{0,4,3,2,1:T(8,128)} copy(f32[4,3,3,3,512]{4,0,2,1,3:T(4,128)S(1)} %fusion.7) | data formatting | bytes 442368 | tf_op jit(solution)/shard_map/concatenate | solution.py:27
  64.3 57.4 %gather_fusion.1 = f32[16384,4]{1,0:T(8,128)} fusion(f32[4,13824]{0,1:T(8,128)} %bitcast.90, s32[16384]{0:T(1024)S(1)} %broadcast_clamp_fusion), kind=kCustom, calls=%fused_computation.clone | custom fusion | bytes 589824 | tf_op jit(solution)/shard_map/jit(_take)/gather | solution.py:41
  121.7 5.2 %copy.26 = f32[32,512,4]{1,0,2:T(8,128)S(1)} copy(f32[32,512,4]{2,1,0:T(8,128)} %bitcast.92) | data formatting | bytes 524288 | tf_op jit(solution)/shard_map/jit(_take)/gather | solution.py:41
  127.1 0.7 fusion.42
  127.8 0.6 multiply_reduce_fusion.6
  128.4 37.9 %all-reduce.2 = (f32[]{:T(128)}, f32[]{:T(128)}, f32[]{:T(128)}) all-reduce(f32[]{:T(128)} %multiply_reduce_fusion.7, f32[]{:T(128)} %multiply_reduce_fusion.6, f32[]{:T(128)} %fusion.42), channel_id=1, replica_groups=mesh['gx'=4,'gy'=4,'gz'=2] {'gx','gy','gz'}, use_global_device_ids=true, to_apply=%region_8.10 | all-reduce | flops 3 | bytes 24 | tf_op jit(solution)/shard_map/psum | solution.py:87
  168.5 0.5 collective-permute-start.7
  169.0 0.1 collective-permute-start.6
  169.1 1.3 collective-permute-done.7
  170.4 2.2 collective-permute-done.6
  172.6 2.3 collective-permute-start.9
  174.9 0.7 collective-permute-start.8
  175.5 1.7 collective-permute-done.9
  177.2 3.2 %collective-permute-done.8 = f32[4,3,1,1,512]{4,0,2,1,3:T(4,128)S(1)} collective-permute-done((f32[4,3,1,1,512]{4,0,2,1,3:T(4,128)S(1)}, f32[4,3,1,1,512]{4,0,2,1,3:T(4,128)S(1)}, u32[]{:S(2)}, u32[]{:S(2)}) %collective-permute-start.8) | collective-permute-done | bytes 24608 | tf_op jit(solution)/shard_map/ppermute | solution.py:25
  180.5 1.5 collective-permute-start.11
  182.0 0.6 collective-permute-start.10
  182.6 2.3 collective-permute-done.11
  184.9 1.4 collective-permute-done.10
  186.4 0.1 fusion.13
  186.4 4.3 %copy.29 = f32[4,3,3,3,512]{0,4,3,2,1:T(8,128)} copy(f32[4,3,3,3,512]{4,0,2,1,3:T(4,128)S(1)} %fusion.13) | data formatting | bytes 442368 | tf_op jit(solution)/shard_map/concatenate | solution.py:27
  190.7 57.4 %gather_fusion.2 = f32[16384,4]{1,0:T(8,128)} fusion(f32[4,13824]{0,1:T(8,128)} %bitcast.89, s32[16384]{0:T(1024)S(1)} %broadcast_clamp_fusion), kind=kCustom, calls=%fused_computation.1.clone | custom fusion | bytes 589824 | tf_op jit(solution)/shard_map/jit(_take)/gather | solution.py:41
  248.1 5.2 %copy.30 = f32[32,512,4]{1,0,2:T(8,128)S(1)} copy(f32[32,512,4]{2,1,0:T(8,128)} %bitcast.91) | data formatting | bytes 524288 | tf_op jit(solution)/shard_map/jit(_take)/gather | solution.py:41
  253.5 0.7 multiply_reduce_fusion.4
  254.2 0.6 fusion.48
  254.8 37.7 %all-reduce.1 = (f32[]{:T(128)}, f32[]{:T(128)}, f32[]{:T(128)}) all-reduce(f32[]{:T(128)} %get-tuple-element.6, f32[]{:T(128)} %multiply_reduce_fusion.4, f32[]{:T(128)} %get-tuple-element.5), channel_id=1, replica_groups=mesh['gx'=4,'gy'=4,'gz'=2] {'gx','gy','gz'}, use_global_device_ids=true, to_apply=%region_16.18 | all-reduce | flops 3 | bytes 24 | tf_op jit(solution)/shard_map/psum | solution.py:87
  294.7 0.6 copy.31
  295.3 0.6 copy.32
  (23 shorter events, 0.4 us)
Async XLA Ops:
  0.6 15.2 %copy-start = (f32[128,128]{1,0:T(8,128)S(1)}, f32[128,128]{1,0:T(8,128)}, u32[]{:S(2)}) copy-start(f32[128,128]{1,0:T(8,128)} %param.19) | copy-start | bytes 196612
  40.1 1.5 collective-permute-start.1
  40.1 3.2 %collective-permute-start = (f32[4,1,1,1,512]{4,0,2,1,3:T(4,128)S(1)}, f32[4,1,1,1,512]{4,0,2,1,3:T(4,128)S(1)}, u32[]{:S(2)}, u32[]{:S(2)}) collective-permute-start(f32[4,1,1,1,512]{4,0,2,1,3:T(4,128)S(1)} %pad_maximum_fusion.7), channel_id=1, source_target_pairs={{0,8},{8,16},{16,24},{24,0},{1,9},{9,17},{17,25},{25,1},{2,10},{10... | collective-permute-start | bytes 24584 | tf_op jit(solution)/shard_map/ppermute | solution.py:25
  44.0 5.2 %collective-permute-start.3 = (f32[4,3,1,1,512]{4,0,2,1,3:T(4,128)S(1)}, f32[4,3,1,1,512]{4,0,2,1,3:T(4,128)S(1)}, u32[]{:S(2)}, u32[]{:S(2)}) collective-permute-start(f32[4,3,1,1,512]{4,0,2,1,3:T(4,128)S(1)} %fusion.35), channel_id=1, source_target_pairs={{2,0},{4,2},{6,4},{0,6},{3,1},{5,3},{7,5},{1,7},{10,8},{12,10},{14... | collective-permute-start | bytes 73736 | tf_op jit(solution)/shard_map/ppermute | solution.py:26
  47.7 5.6 %collective-permute-start.2 = (f32[4,3,1,1,512]{4,0,2,1,3:T(4,128)S(1)}, f32[4,3,1,1,512]{4,0,2,1,3:T(4,128)S(1)}, u32[]{:S(2)}, u32[]{:S(2)}) collective-permute-start(f32[4,3,1,1,512]{4,0,2,1,3:T(4,128)S(1)} %fusion.35), channel_id=1, source_target_pairs={{0,2},{2,4},{4,6},{6,0},{1,3},{3,5},{5,7},{7,1},{8,10},{10,12},{12... | collective-permute-start | bytes 73736 | tf_op jit(solution)/shard_map/ppermute | solution.py:25
  54.0 4.4 %collective-permute-start.5 = (f32[4,3,3,1,512]{4,0,2,1,3:T(4,128)S(1)}, f32[4,3,3,1,512]{4,0,2,1,3:T(4,128)S(1)}, u32[]{:S(2)}, u32[]{:S(2)}) collective-permute-start(f32[4,3,3,1,512]{4,0,2,1,3:T(4,128)S(1)} %fusion.17), channel_id=1, source_target_pairs={{1,0},{0,1},{3,2},{2,3},{5,4},{4,5},{7,6},{6,7},{9,8},{8,9},{11,10... | collective-permute-start | bytes 221192 | tf_op jit(solution)/shard_map/ppermute | solution.py:26
  54.6 4.6 %collective-permute-start.4 = (f32[4,3,3,1,512]{4,0,2,1,3:T(4,128)S(1)}, f32[4,3,3,1,512]{4,0,2,1,3:T(4,128)S(1)}, u32[]{:S(2)}, u32[]{:S(2)}) collective-permute-start(f32[4,3,3,1,512]{4,0,2,1,3:T(4,128)S(1)} %fusion.17), channel_id=1, source_target_pairs={{0,1},{1,0},{2,3},{3,2},{4,5},{5,4},{6,7},{7,6},{8,9},{9,8},{10,11... | collective-permute-start | bytes 221192 | tf_op jit(solution)/shard_map/ppermute | solution.py:25
  59.9 67.1 %copy-start.1 = (s32[1,1,1,32,512]{4,3,2,1,0:T(8,128)S(1)}, s32[1,1,1,32,512]{4,3,2,1,0:T(8,128)}, u32[]{:S(2)}) copy-start(s32[1,1,1,32,512]{4,3,2,1,0:T(8,128)} %param.15) | copy-start | bytes 196612
  60.0 67.1 %copy-start.2 = (f32[1,1,1,512]{3,2,1,0:T(1,128)S(1)}, f32[1,1,1,512]{3,2,1,0:T(1,128)}, u32[]{:S(2)}) copy-start(f32[1,1,1,512]{3,2,1,0:T(1,128)} %param.13) | copy-start | bytes 6148
  60.0 67.2 %copy-start.3 = (f32[3,1,1,1,512]{4,3,2,1,0:T(1,128)S(1)}, f32[3,1,1,1,512]{4,3,2,1,0:T(1,128)}, u32[]{:S(2)}) copy-start(f32[3,1,1,1,512]{4,3,2,1,0:T(1,128)} %param.12) | copy-start | bytes 18436
  168.5 1.9 collective-permute-start.7
  169.0 3.6 %collective-permute-start.6 = (f32[4,1,1,1,512]{4,0,2,1,3:T(4,128)S(1)}, f32[4,1,1,1,512]{4,0,2,1,3:T(4,128)S(1)}, u32[]{:S(2)}, u32[]{:S(2)}) collective-permute-start(f32[4,1,1,1,512]{4,0,2,1,3:T(4,128)S(1)} %pad_maximum_fusion.6), channel_id=1, source_target_pairs={{0,8},{8,16},{16,24},{24,0},{1,9},{9,17},{17,25},{25,1},{2,10},{10... | collective-permute-start | bytes 24584 | tf_op jit(solution)/shard_map/ppermute | solution.py:25
  172.6 4.6 %collective-permute-start.9 = (f32[4,3,1,1,512]{4,0,2,1,3:T(4,128)S(1)}, f32[4,3,1,1,512]{4,0,2,1,3:T(4,128)S(1)}, u32[]{:S(2)}, u32[]{:S(2)}) collective-permute-start(f32[4,3,1,1,512]{4,0,2,1,3:T(4,128)S(1)} %fusion.37), channel_id=1, source_target_pairs={{2,0},{4,2},{6,4},{0,6},{3,1},{5,3},{7,5},{1,7},{10,8},{12,10},{14... | collective-permute-start | bytes 73736 | tf_op jit(solution)/shard_map/ppermute | solution.py:26
  174.9 5.6 %collective-permute-start.8 = (f32[4,3,1,1,512]{4,0,2,1,3:T(4,128)S(1)}, f32[4,3,1,1,512]{4,0,2,1,3:T(4,128)S(1)}, u32[]{:S(2)}, u32[]{:S(2)}) collective-permute-start(f32[4,3,1,1,512]{4,0,2,1,3:T(4,128)S(1)} %fusion.37), channel_id=1, source_target_pairs={{0,2},{2,4},{4,6},{6,0},{1,3},{3,5},{5,7},{7,1},{8,10},{10,12},{12... | collective-permute-start | bytes 73736 | tf_op jit(solution)/shard_map/ppermute | solution.py:25
  180.5 4.4 %collective-permute-start.11 = (f32[4,3,3,1,512]{4,0,2,1,3:T(4,128)S(1)}, f32[4,3,3,1,512]{4,0,2,1,3:T(4,128)S(1)}, u32[]{:S(2)}, u32[]{:S(2)}) collective-permute-start(f32[4,3,3,1,512]{4,0,2,1,3:T(4,128)S(1)} %fusion.21), channel_id=1, source_target_pairs={{1,0},{0,1},{3,2},{2,3},{5,4},{4,5},{7,6},{6,7},{9,8},{8,9},{11,10... | collective-permute-start | bytes 221192 | tf_op jit(solution)/shard_map/ppermute | solution.py:26
  182.0 4.4 %collective-permute-start.10 = (f32[4,3,3,1,512]{4,0,2,1,3:T(4,128)S(1)}, f32[4,3,3,1,512]{4,0,2,1,3:T(4,128)S(1)}, u32[]{:S(2)}, u32[]{:S(2)}) collective-permute-start(f32[4,3,3,1,512]{4,0,2,1,3:T(4,128)S(1)} %fusion.21), channel_id=1, source_target_pairs={{0,1},{1,0},{2,3},{3,2},{4,5},{5,4},{6,7},{7,6},{8,9},{9,8},{10,11... | collective-permute-start | bytes 221192 | tf_op jit(solution)/shard_map/ppermute | solution.py:25
where the time goes:
time: 297 us; the launch traced here: 296 us
  local copies, waits for them, and re-layouts  143 us (48%)
  blocking collectives  89.8 us (30%)
  other arithmetic  24.8 us (8%)
  waiting for transfers between devices  20.4 us (7%)
  starting transfers between devices  11.8 us (4%)
  between operations  5.87 us (2%)
    gather x4, local copies, waits for them, and re-layouts, pair_forces(): partner = jnp.take(neighbourhood, neighbour_rows, axis=1)  125 us
    psum x2, blocking collectives, shards(): lax.psum((jnp.sum(forces * speeds), jnp.sum(speeds * speeds), jnp.sum(for...  75.6 us
    ppermute x6, waiting for transfers between devices, with_halo(): before = lax.ppermute(last, axis, up)  13.5 us
    scatter-add x1, other arithmetic, relax_events(): jnp.zeros_like(group_positions).at[:, flattened].add(shifted.reshape(3, -1))  11.6 us
    unnamed x1, blocking collectives  8.64 us
    concatenate x2, local copies, waits for them, and re-layouts, with_halo(): x = jnp.concatenate([before, x, after], axis=dim)  8.61 us
    ppermute x6, starting transfers between devices, with_halo(): after = lax.ppermute(leading, axis, down)  8.54 us
    ppermute x6, waiting for transfers between devices, with_halo(): after = lax.ppermute(leading, axis, down)  6.96 us
  transfers between devices with their start and end apart: 12, of which 11 were waited for; matrix products, arithmetic and copies ran while one was open for 1% of the time, Pallas kernels for 0%

commit v1 on v0

v1 whole, which is shorter than its diff:
```python
import functools

import jax
import jax.numpy as jnp
from jax import lax
from jax.experimental import pallas as pl
from jax.experimental.pallas import tpu as pltpu
from jax.sharding import PartitionSpec as P

width_scale = 1.5
time_step = 0.1
mixing = 0.1
epsilon = 1e-06

MESH = pl.DeviceIdType.MESH
LANES = 128
ROWS = 16
DIRECT = 64


def lane_gather(table, index):
    return jnp.take_along_axis(table, index, axis=1, mode="promise_in_bounds")


def cycle_kernel(
    mesh_shape,
    pos_in,
    vel_in,
    eps_in,
    nbr_in,
    live_in,
    count_in,
    atoms_in,
    weight_in,
    map_in,
    pos_out,
    vel_out,
    pos_v,
    vel_v,
    eps_v,
    nbr,
    live,
    count_v,
    atoms,
    weight_v,
    tmap,
    col,
    moved,
    shifts,
    table,
    table2,
    speeds,
    forces,
    forces2,
    sums,
    local_sem,
    col_sem,
    send_sem,
    recv_sem,
    sum_send,
    sum_recv,
):
    nx, ny, nz = mesh_shape
    devices = nx * ny * nz
    x, y, z = lax.axis_index("gx"), lax.axis_index("gy"), lax.axis_index("gz")
    slots, atom_count = nbr.shape
    events, template = atoms.shape[1:]
    chunks = atom_count // LANES
    home = 13
    depth_offsets = (0, 1) if nz == 2 else (0, 1, 2)
    depths = len(depth_offsets)

    def peer(dx, dy, dz):
        return (
            lax.rem(x + dx + nx, nx),
            lax.rem(y + dy + ny, ny),
            lax.rem(z + dz + nz, nz),
        )

    def copies(j):
        dirs = [j] if nz > 2 or j % 3 != 0 else [j, j + 2]
        return [s for d in dirs for s in range(d, slots, 27)]

    around = [
        (a, b, c)
        for a in range(3)
        for b in range(3)
        for c in depth_offsets
        if (a, b, c) != (1, 1, 1)
    ]
    beside = [(a, b) for a in range(3) for b in range(3) if (a, b) != (1, 1)]
    if devices <= DIRECT:
        stages = [
            [
                (dx, dy, dz)
                for dx in range(nx)
                for dy in range(ny)
                for dz in range(nz)
                if (dx, dy, dz) != (0, 0, 0)
            ]
        ]
    else:
        stages = [
            [(d, 0, 0) for d in range(1, nx)],
            [(0, d, 0) for d in range(1, ny)],
            [(0, 0, d) for d in range(1, nz)],
        ]
    greeted = {((1 - a) % nx, (1 - b) % ny, (1 - c) % nz) for a, b, c in around}
    greeted |= {((a - 1) % nx, (b - 1) % ny, (c - 1) % nz) for a, b, c in around}
    greeted |= {offset for stage in stages for offset in stage}
    greeted |= {(0, 0, d) for d in range(1, nz)}
    greeted = sorted(greeted)

    own_atoms = atoms.at[z]
    pairs = [
        (pos_in, pos_v),
        (vel_in, vel_v),
        (eps_in, eps_v),
        (count_in, count_v),
        (weight_in, weight_v),
        (atoms_in, own_atoms),
        (map_in, tmap),
        (nbr_in, nbr),
        (live_in, live),
    ]
    loads = [
        pltpu.make_async_copy(src, dst, local_sem.at[i]) for i, (src, dst) in enumerate(pairs)
    ]
    for load in loads:
        load.start()
    barrier = pltpu.get_barrier_semaphore()
    for offset in greeted:
        pl.semaphore_signal(barrier, inc=1, device_id=peer(*offset), device_id_type=MESH)
    for load in loads[:6]:
        load.wait()

    for chunk in range(chunks):
        lanes = pl.ds(chunk * LANES, LANES)
        for i in range(3):
            row = i * chunks + chunk
            col[z, pl.ds(row, 1), :] = pos_v[i, :, lanes]
            speeds[pl.ds(home * ROWS + row, 1), :] = vel_v[i, :, lanes]
        row = 3 * chunks + chunk
        col[z, pl.ds(row, 1), :] = jnp.sqrt(eps_v[:, lanes])
        speeds[pl.ds(home * ROWS + row, 1), :] = jnp.zeros((1, LANES), jnp.float32)
    alive = lax.broadcasted_iota(jnp.int32, (1, events), 1) < count_v[...]
    live_weight = jnp.where(alive, weight_v[...], 0.0)
    spread = jnp.broadcast_to(live_weight, (events, events))
    diagonal = lax.broadcasted_iota(jnp.int32, (events, events), 0) == lax.broadcasted_iota(
        jnp.int32, (events, events), 1
    )
    column_weight = jnp.sum(jnp.where(diagonal, spread, 0.0), axis=1, keepdims=True)
    col[z, pl.ds(ROWS, events), :] = jnp.broadcast_to(column_weight, (events, LANES))

    pl.semaphore_wait(barrier, len(greeted))

    column_copies = []
    for d in range(1, nz):
        for part, ref in enumerate((col, atoms)):
            copy = pltpu.make_async_remote_copy(
                src_ref=ref.at[z],
                dst_ref=ref.at[z],
                send_sem=col_sem.at[0, part, d - 1],
                recv_sem=col_sem.at[1, part, d - 1],
                device_id=peer(0, 0, d),
                device_id_type=MESH,
            )
            copy.start()
            column_copies.append(copy)

    def send_around(ref, which):
        for a, b, c in around:
            j = (a * 3 + b) * 3 + c
            pltpu.make_async_remote_copy(
                src_ref=ref.at[pl.ds(home * ROWS, ROWS)],
                dst_ref=ref.at[pl.ds(j * ROWS, ROWS)],
                send_sem=send_sem.at[which],
                recv_sem=recv_sem.at[which],
                device_id=peer(1 - a, 1 - b, 1 - c),
                device_id_type=MESH,
            ).start()

    def wait_total(ref, rows, sem):
        part = ref.at[pl.ds(0, rows)]
        pltpu.make_async_copy(part, part, sem).wait()

    send_around(speeds, 0)
    for load in loads[6:]:
        load.wait()
    for copy in column_copies:
        copy.wait_recv()

    total_events = nz * events
    members = atoms[...].reshape(total_events, template)
    member_chunk = lax.shift_right_logical(members, 7)
    member_lane = members & (LANES - 1)
    weights = jnp.concatenate([col[d, pl.ds(ROWS, events), :] for d in range(nz)], axis=0)
    centred = []
    for i in range(3):
        taken = jnp.zeros((total_events, template), jnp.float32)
        for d in range(nz):
            for chunk in range(chunks):
                source = jnp.broadcast_to(
                    col[d, pl.ds(i * chunks + chunk, 1), :], (total_events, LANES)
                )
                picked = lane_gather(source, member_lane)
                taken = jnp.where(member_chunk == d * chunks + chunk, picked, taken)
        mean = jnp.sum(taken, axis=1, keepdims=True) * (1.0 / template)
        centred.append(taken - mean)
    shifted = jnp.dot(
        jnp.concatenate(centred, axis=0),
        tmap[...],
        precision=lax.Precision.HIGHEST,
        preferred_element_type=jnp.float32,
    )
    for i in range(3):
        shift = shifted[i * total_events : (i + 1) * total_events] * weights
        coarse = shift.astype(jnp.bfloat16).astype(jnp.float32)
        shifts[i] = coarse
        shifts[3 + i] = shift - coarse

    column_chunks = nz * chunks
    lane_row = lax.broadcasted_iota(jnp.int32, (LANES, template), 0)
    chunk_row = lax.broadcasted_iota(jnp.int32, (column_chunks, template), 0)
    summed = jnp.zeros((6 * column_chunks, LANES), jnp.float32)
    for first in range(0, total_events, 2):
        left, right = [], []
        for e in range(first, first + 2):
            here = member_chunk[e : e + 1] == chunk_row
            left.append(
                jnp.concatenate(
                    [
                        jnp.where(here, shifts[q, pl.ds(e, 1), :], 0.0)
                        for q in range(6)
                    ],
                    axis=0,
                )
            )
            right.append(jnp.where(member_lane[e : e + 1] == lane_row, 1.0, 0.0))
        summed = summed + lax.dot_general(
            jnp.concatenate(left, axis=1).astype(jnp.bfloat16),
            jnp.concatenate(right, axis=1).astype(jnp.bfloat16),
            (((1,), (1,)), ((), ())),
            preferred_element_type=jnp.float32,
        )
    half = 3 * column_chunks
    displaced = summed[:half] + summed[half:]
    for d in range(nz):
        pieces = [
            displaced[i * column_chunks + d * chunks : i * column_chunks + (d + 1) * chunks]
            for i in range(3)
        ]
        pieces.append(jnp.zeros((chunks, LANES), jnp.float32))
        moved[d] = col[d, pl.ds(0, ROWS), :] + jnp.concatenate(pieces, axis=0)

    for c in range(3):
        table[pl.ds((home - 1 + c) * ROWS, ROWS), :] = moved[lax.rem(z + c - 1 + nz, nz)]
    for a, b in beside:
        pltpu.make_async_remote_copy(
            src_ref=table.at[pl.ds((home - 1) * ROWS, depths * ROWS)],
            dst_ref=table.at[pl.ds((a * 3 + b) * 3 * ROWS, depths * ROWS)],
            send_sem=send_sem.at[1],
            recv_sem=recv_sem.at[1],
            device_id=peer(1 - a, 1 - b, 0),
            device_id_type=MESH,
        ).start()
    wait_total(table, len(beside) * depths * ROWS, recv_sem.at[1])
    for a, b in beside:
        for c in depth_offsets:
            j = (a * 3 + b) * 3 + c
            block = table[pl.ds(j * ROWS, ROWS), :]
            for s in copies(j)[1:]:
                table[pl.ds(s * ROWS, ROWS), :] = block
    for c in range(3):
        j = home - 1 + c
        for s in range(j + 27, slots, 27):
            table[pl.ds(s * ROWS, ROWS), :] = table[pl.ds(j * ROWS, ROWS), :]

    def pair_forces(where, result):
        total = [[jnp.zeros((8, LANES), jnp.float32)] * 3 for _ in range(chunks)]
        for group in range(slots // 8):
            source = [
                [
                    where[pl.ds(group * 8 * ROWS + i * chunks + t, 8, stride=ROWS), :]
                    for t in range(chunks)
                ]
                for i in range(4)
            ]
            for chunk in range(chunks):
                rows, lanes = pl.ds(group * 8, 8), pl.ds(chunk * LANES, LANES)
                index = nbr[rows, lanes]
                lane, part = index & (LANES - 1), lax.shift_right_logical(index, 7)
                partner = []
                for i in range(4):
                    picked = lane_gather(source[i][0], lane)
                    for t in range(1, chunks):
                        picked = jnp.where(part == t, lane_gather(source[i][t], lane), picked)
                    partner.append(picked)
                own = [
                    where[pl.ds(home * ROWS + i * chunks + chunk, 1), :] for i in range(4)
                ]
                apart = [own[i] - partner[i] for i in range(3)]
                square = apart[0] * apart[0] + apart[1] * apart[1] + apart[2] * apart[2]
                strength = (
                    own[3]
                    * partner[3]
                    * live[rows, lanes].astype(jnp.float32)
                    * jnp.exp(square * (-0.5 / (width_scale * width_scale)))
                    * (1.0 / (width_scale * width_scale))
                )
                total[chunk] = [total[chunk][i] + strength * apart[i] for i in range(3)]
        for chunk in range(chunks):
            for i in range(3):
                result[pl.ds(home * ROWS + i * chunks + chunk, 1), :] = jnp.sum(
                    total[chunk][i], axis=0, keepdims=True
                )
        result[pl.ds(home * ROWS + 3 * chunks, chunks), :] = jnp.zeros(
            (chunks, LANES), jnp.float32
        )

    def whole(value):
        return jnp.sum(jnp.sum(value, axis=0, keepdims=True), axis=1, keepdims=True)

    lane_index = lax.broadcasted_iota(jnp.int32, (1, LANES), 1)
    most = max(len(stage) for stage in stages) + 1

    def sum_start(force, speed, which):
        row = jnp.where(lane_index == 0, whole(force * speed), 0.0)
        row = jnp.where(lane_index == 1, whole(speed * speed), row)
        row = jnp.where(lane_index == 2, whole(force * force), row)
        return stage_start(row, which, 0)

    def stage_start(row, which, s):
        base = (which * len(stages) + s) * most
        sums[base] = row
        for slot, offset in enumerate(stages[s]):
            pltpu.make_async_remote_copy(
                src_ref=sums.at[base],
                dst_ref=sums.at[base + 1 + slot],
                send_sem=sum_send.at[which, s],
                recv_sem=sum_recv.at[which, s],
                device_id=peer(*offset),
                device_id_type=MESH,
            ).start()

    def sum_finish(which):
        for s, stage in enumerate(stages):
            base = (which * len(stages) + s) * most
            wait_total(sums, len(stage), sum_recv.at[which, s])
            row = jnp.sum(sums[pl.ds(base, len(stage) + 1)], axis=0)
            if s + 1 < len(stages):
                stage_start(row, which, s + 1)
        power, speed_sq, force_sq = row[:, 0:1], row[:, 1:2], row[:, 2:3]
        cosine = power / (jnp.sqrt(speed_sq + epsilon) * jnp.sqrt(force_sq + epsilon))
        ratio = jnp.sqrt((speed_sq + epsilon) / (force_sq + epsilon))
        keep = 0.5 * (1.0 + cosine)
        return keep * (1.0 - mixing), keep * mixing * ratio + time_step

    def block(ref, j):
        return ref[pl.ds(j * ROWS, ROWS), :]

    pair_forces(table, forces)
    send_around(forces, 2)
    sum_start(block(forces, home), block(speeds, home), 0)
    wait_total(speeds, len(around) * ROWS, recv_sem.at[0])
    old, new = sum_finish(0)
    wait_total(forces, len(around) * ROWS, recv_sem.at[2])
    for a, b, c in around + [(1, 1, 1)]:
        j = (a * 3 + b) * 3 + c
        later = block(table, j) + time_step * (
            old * block(speeds, j) + new * block(forces, j)
        )
        for s in copies(j):
            table2[pl.ds(s * ROWS, ROWS), :] = later
    speed = old * block(speeds, home) + new * block(forces, home)

    pair_forces(table2, forces2)
    force = block(forces2, home)
    sum_start(force, speed, 1)
    old, new = sum_finish(1)
    speed = old * speed + new * force
    place = block(table2, home) + time_step * speed
    for chunk in range(chunks):
        lanes = pl.ds(chunk * LANES, LANES)
        for i in range(3):
            row = i * chunks + chunk
            pos_out[i, :, lanes] = place[row : row + 1]
            vel_out[i, :, lanes] = speed[row : row + 1]

    for copy in column_copies:
        copy.wait_send()
    wait_total(speeds, len(around) * ROWS, send_sem.at[0])
    wait_total(table, len(beside) * depths * ROWS, send_sem.at[1])
    wait_total(forces, len(around) * ROWS, send_sem.at[2])
    for which in range(2):
        for s, stage in enumerate(stages):
            wait_total(sums, len(stage), sum_send.at[which, s])


def shards(
    mesh_shape,
    positions,
    velocity,
    atom_eps,
    neighbours,
    pair_live,
    event_count,
    event_atoms,
    event_weight,
    template_map,
):
    atom_count = positions.shape[4]
    slots = neighbours.shape[3]
    events, template = event_atoms.shape[3:]
    nx, ny, nz = mesh_shape
    devices = nx * ny * nz
    stages, most = (1, devices) if devices <= DIRECT else (3, max(mesh_shape))
    f32, i32 = jnp.float32, jnp.int32
    blocks = pltpu.VMEM((slots * ROWS, LANES), f32)
    outs = pl.pallas_call(
        functools.partial(cycle_kernel, mesh_shape),
        out_shape=[jax.ShapeDtypeStruct((3, 1, atom_count), f32)] * 2,
        in_specs=[pl.BlockSpec(memory_space=pl.ANY)] * 9,
        out_specs=[pl.BlockSpec(memory_space=pltpu.VMEM)] * 2,
        scratch_shapes=[
            pltpu.VMEM((3, 1, atom_count), f32),
            pltpu.VMEM((3, 1, atom_count), f32),
            pltpu.VMEM((1, atom_count), f32),
            pltpu.VMEM((slots, atom_count), i32),
            pltpu.VMEM((slots, atom_count), i32),
            pltpu.VMEM((1, 1), i32),
            pltpu.VMEM((nz, events, template), i32),
            pltpu.VMEM((1, events), f32),
            pltpu.VMEM((template, template), f32),
            pltpu.VMEM((nz, ROWS + events, LANES), f32),
            pltpu.VMEM((nz, ROWS, LANES), f32),
            pltpu.VMEM((6, nz * events, template), f32),
            blocks,
            blocks,
            blocks,
            blocks,
            blocks,
            pltpu.VMEM((2 * stages * most, 1, LANES), f32),
            pltpu.SemaphoreType.DMA((9,)),
            pltpu.SemaphoreType.DMA((2, 2, nz - 1)),
            pltpu.SemaphoreType.DMA((3,)),
            pltpu.SemaphoreType.DMA((3,)),
            pltpu.SemaphoreType.DMA((2, stages)),
            pltpu.SemaphoreType.DMA((2, stages)),
        ],
        compiler_params=pltpu.CompilerParams(
            collective_id=0, has_side_effects=True, vmem_limit_bytes=32 * 1024 * 1024
        ),
        cost_estimate=pl.CostEstimate(flops=10**7, bytes_accessed=10**6, transcendentals=10**5),
    )(
        positions.reshape(3, 1, atom_count),
        velocity.reshape(3, 1, atom_count),
        atom_eps.reshape(1, atom_count),
        neighbours.reshape(slots, atom_count),
        pair_live.reshape(slots, atom_count),
        event_count.reshape(1, 1),
        event_atoms.reshape(events, template),
        event_weight.reshape(1, events),
        template_map,
    )
    return tuple(out.reshape(positions.shape) for out in outs)


def solution(mesh):
    in_specs = (
        P(None, "gx", "gy", "gz", None),
        P(None, "gx", "gy", "gz", None),
        P("gx", "gy", "gz", None),
        P("gx", "gy", "gz", None, None),
        P("gx", "gy", "gz", None, None),
        P("gx", "gy", "gz"),
        P("gx", "gy", "gz", None, None),
        P("gx", "gy", "gz", None),
        P(),
    )
    out_specs = (P(None, "gx", "gy", "gz", None), P(None, "gx", "gy", "gz", None))
    mesh_shape = tuple(mesh.shape[axis] for axis in ("gx", "gy", "gz"))
    return jax.shard_map(
        functools.partial(shards, mesh_shape),
        mesh=mesh,
        in_specs=in_specs,
        out_specs=out_specs,
        check_vma=False,
    )
```

time: 297 us -> 33.7 us (0.11)
  local copies, waits for them, and re-layouts: 143 us -> 5.08 us
  blocking collectives: 89.8 us -> 0 us
  Pallas kernels: 0 us -> 26.9 us
  other arithmetic: 24.8 us -> 0 us
  waiting for transfers between devices: 20.4 us -> 0 us
  starting transfers between devices: 11.8 us -> 0 us
  between operations: 5.87 us -> 1.35 us
    gather x6 -> x0, local copies, waits for them, and re-layouts: 131 us -> none  [the longest x4 125 us: pair_forces(): partner = jnp.take(neighbourhood, neighbour_rows, axis=1)]
    psum x2 -> x0, blocking collectives: 75.6 us -> none  [shards(): lax.psum((jnp.sum(forces * speeds), jnp.sum(speeds * speeds), jnp.sum(for...]
    pallas_call x0 -> x1, Pallas kernels: none -> 26.9 us  [shards(): pl.pallas_call(functools.partial(cycle_kernel, mesh_shape), out_shape=[ja...]
    ppermute x12 -> x0, waiting for transfers between devices: 20.4 us -> none  [the longest x6 13.5 us: with_halo(): before = lax.ppermute(last, axis, up)]
    ppermute x12 -> x0, starting transfers between devices: 11.8 us -> none  [the longest x6 8.54 us: with_halo(): after = lax.ppermute(leading, axis, down)]
    scatter-add x1 -> x0, other arithmetic: 11.6 us -> none  [relax_events(): jnp.zeros_like(group_positions).at[:, flattened].add(shifted.reshape(3, -1))]
    unnamed x1 -> x0, blocking collectives: 8.64 us -> none
    concatenate x2 -> x0, local copies, waits for them, and re-layouts: 8.61 us -> none  [with_halo(): x = jnp.concatenate([before, x, after], axis=dim)]
  transfers between devices with their start and end apart: 12 -> 0, of which waited for: 11 -> 0; matrix products, arithmetic and copies ran while one was open for 1% -> 0% of each run, Pallas kernels for 0% -> 0%
where the time goes in v1:
time: 33.7 us; the launch traced here: 33.3 us
  Pallas kernels  26.9 us (80%)
  local copies, waits for them, and re-layouts  5.08 us (15%)
  between operations  1.35 us (4%)
    pallas_call x1, Pallas kernels, shards(): pl.pallas_call(functools.partial(cycle_kernel, mesh_shape), out_shape=[ja...  26.9 us
    unnamed x18, local copies, waits for them, and re-layouts  5.08 us

profile of v1, /device:TPU:0, one launch (start us, length us, event | category | flops | bytes accessed | tf_op | source)
XLA Modules:
  0.0 33.3 jit_solution(11243999191800427611)
XLA Ops:
  0.6 0.0 copy-start.6
  1.3 0.0 copy-start.3
  1.3 0.0 copy-start.4
  1.3 0.0 copy-start.7
  1.3 0.0 copy-done.6
  1.3 0.7 %copy-done.3 = s32[1,1,1,16,128]{4,3,2,1,0:T(8,128)S(1)} copy-done((s32[1,1,1,16,128]{4,3,2,1,0:T(8,128)S(1)}, s32[1,1,1,16,128]{4,3,2,1,0:T(8,128)}, u32[]{:S(2)}) %copy-start.3) | copy-done | bytes 8216
  2.0 0.0 copy-done.4
  2.0 0.0 copy-done.7
  2.0 0.0 copy-start
  2.0 0.8 %copy-done = s32[1,1,1,32,512]{4,3,2,1,0:T(8,128)S(1)} copy-done((s32[1,1,1,32,512]{4,3,2,1,0:T(8,128)S(1)}, s32[1,1,1,32,512]{4,3,2,1,0:T(8,128)}, u32[]{:S(2)}) %copy-start) | copy-done | bytes 65560
  2.9 0.0 copy-start.1
  2.9 0.8 %copy-done.1 = s32[1,1,1,32,512]{4,3,2,1,0:T(8,128)S(1)} copy-done((s32[1,1,1,32,512]{4,3,2,1,0:T(8,128)S(1)}, s32[1,1,1,32,512]{4,3,2,1,0:T(8,128)}, u32[]{:S(2)}) %copy-start.1) | copy-done | bytes 65560
  3.7 0.0 copy-start.2
  3.7 0.8 %copy-done.2 = f32[128,128]{1,0:T(8,128)S(1)} copy-done((f32[128,128]{1,0:T(8,128)S(1)}, f32[128,128]{1,0:T(8,128)}, u32[]{:S(2)}) %copy-start.2) | copy-done | bytes 65560
  4.5 0.0 copy-start.5
  4.5 0.7 %copy-done.5 = f32[3,1,1,1,512]{4,3,2,1,0:T(1,128)S(1)} copy-done((f32[3,1,1,1,512]{4,3,2,1,0:T(1,128)S(1)}, f32[3,1,1,1,512]{4,3,2,1,0:T(1,128)}, u32[]{:S(2)}) %copy-start.5) | copy-done | bytes 6168
  5.2 26.9 %shard_map.104 = (f32[3,1,512]{2,1,0:T(1,128)S(1)}, f32[3,1,512]{2,1,0:T(1,128)S(1)}) custom-call(f32[3,1,512]{2,1,0:T(1,128)S(1)} %bitcast.18, f32[3,1,512]{2,1,0:T(1,128)S(1)} %bitcast.19, f32[1,512]{1,0:T(1,128)S(1)} %bitcast.22, s32[32,512]{1,0:T(8,128)S(1)} %bitcast.15, s32[32,512]{1,0:T(8,128)S(1)} %bitcast.16, s32[1,1]{1,0:T(1,128)} %bitcast.14.count_in, ...), custom_call_target="tpu_custom_call" | custom-call | flops 10000000 | bytes 1000000 | tf_op jit(solution)/shard_map/pallas_call | solution.py:420
  32.1 0.6 %copy.16 = f32[3,1,1,1,512]{4,3,2,1,0:T(1,128)} copy(f32[3,1,1,1,512]{4,3,2,1,0:T(1,128)S(1)} %bitcast.21) | data formatting | bytes 12288
  32.7 0.6 %copy.17 = f32[3,1,1,1,512]{4,3,2,1,0:T(1,128)} copy(f32[3,1,1,1,512]{4,3,2,1,0:T(1,128)S(1)} %bitcast.20) | data formatting | bytes 12288
Async XLA Ops:
  0.6 0.7 %copy-start.6 = (f32[1,1,1,512]{3,2,1,0:T(1,128)S(1)}, f32[1,1,1,512]{3,2,1,0:T(1,128)}, u32[]{:S(2)}) copy-start(f32[1,1,1,512]{3,2,1,0:T(1,128)} %param.11) | copy-start | bytes 6148
  1.3 0.7 %copy-start.3 = (s32[1,1,1,16,128]{4,3,2,1,0:T(8,128)S(1)}, s32[1,1,1,16,128]{4,3,2,1,0:T(8,128)}, u32[]{:S(2)}) copy-start(s32[1,1,1,16,128]{4,3,2,1,0:T(8,128)} %param.15) | copy-start | bytes 24580
  1.3 0.7 %copy-start.4 = (f32[3,1,1,1,512]{4,3,2,1,0:T(1,128)S(1)}, f32[3,1,1,1,512]{4,3,2,1,0:T(1,128)}, u32[]{:S(2)}) copy-start(f32[3,1,1,1,512]{4,3,2,1,0:T(1,128)} %param.9) | copy-start | bytes 18436
  1.3 0.7 %copy-start.7 = (f32[1,1,1,16]{3,2,1,0:T(1,128)S(1)}, f32[1,1,1,16]{3,2,1,0:T(1,128)}, u32[]{:S(2)}) copy-start(f32[1,1,1,16]{3,2,1,0:T(1,128)} %param.16) | copy-start | bytes 196
  2.0 0.8 %copy-start = (s32[1,1,1,32,512]{4,3,2,1,0:T(8,128)S(1)}, s32[1,1,1,32,512]{4,3,2,1,0:T(8,128)}, u32[]{:S(2)}) copy-start(s32[1,1,1,32,512]{4,3,2,1,0:T(8,128)} %param.12) | copy-start | bytes 196612
  2.9 0.8 %copy-start.1 = (s32[1,1,1,32,512]{4,3,2,1,0:T(8,128)S(1)}, s32[1,1,1,32,512]{4,3,2,1,0:T(8,128)}, u32[]{:S(2)}) copy-start(s32[1,1,1,32,512]{4,3,2,1,0:T(8,128)} %param.13) | copy-start | bytes 196612
  3.7 0.8 %copy-start.2 = (f32[128,128]{1,0:T(8,128)S(1)}, f32[128,128]{1,0:T(8,128)}, u32[]{:S(2)}) copy-start(f32[128,128]{1,0:T(8,128)} %map_in.1) | copy-start | bytes 196612
  4.5 0.7 %copy-start.5 = (f32[3,1,1,1,512]{4,3,2,1,0:T(1,128)S(1)}, f32[3,1,1,1,512]{4,3,2,1,0:T(1,128)}, u32[]{:S(2)}) copy-start(f32[3,1,1,1,512]{4,3,2,1,0:T(1,128)} %param.10) | copy-start | bytes 18436

commit v2 on v1

--- a/solution.py
+++ b/solution.py
@@ -14,6 +14,7 @@
 
 MESH = pl.DeviceIdType.MESH
 LANES = 128
+COORDS = 12
 ROWS = 16
 DIRECT = 64
 
@@ -29,7 +30,6 @@
     eps_in,
     nbr_in,
     live_in,
-    count_in,
     atoms_in,
     weight_in,
     map_in,
@@ -40,13 +40,12 @@
     eps_v,
     nbr,
     live,
-    count_v,
     atoms,
-    weight_v,
     tmap,
     col,
     moved,
     shifts,
+    lanes_hot,
     table,
     table2,
     speeds,
@@ -116,8 +115,7 @@
         (pos_in, pos_v),
         (vel_in, vel_v),
         (eps_in, eps_v),
-        (count_in, count_v),
-        (weight_in, weight_v),
+        (weight_in, col.at[z, pl.ds(ROWS, weight_in.shape[0])]),
         (atoms_in, own_atoms),
         (map_in, tmap),
         (nbr_in, nbr),
@@ -131,7 +129,7 @@
     barrier = pltpu.get_barrier_semaphore()
     for offset in greeted:
         pl.semaphore_signal(barrier, inc=1, device_id=peer(*offset), device_id_type=MESH)
-    for load in loads[:6]:
+    for load in loads[:5]:
         load.wait()
 
     for chunk in range(chunks):
@@ -142,16 +140,7 @@
             speeds[pl.ds(home * ROWS + row, 1), :] = vel_v[i, :, lanes]
         row = 3 * chunks + chunk
         col[z, pl.ds(row, 1), :] = jnp.sqrt(eps_v[:, lanes])
-        speeds[pl.ds(home * ROWS + row, 1), :] = jnp.zeros((1, LANES), jnp.float32)
-    alive = lax.broadcasted_iota(jnp.int32, (1, events), 1) < count_v[...]
-    live_weight = jnp.where(alive, weight_v[...], 0.0)
-    spread = jnp.broadcast_to(live_weight, (events, events))
-    diagonal = lax.broadcasted_iota(jnp.int32, (events, events), 0) == lax.broadcasted_iota(
-        jnp.int32, (events, events), 1
-    )
-    column_weight = jnp.sum(jnp.where(diagonal, spread, 0.0), axis=1, keepdims=True)
-    col[z, pl.ds(ROWS, events), :] = jnp.broadcast_to(column_weight, (events, LANES))
-
+        speeds[pl.ds(home * ROWS + row, 1), :] = col[z, pl.ds(row, 1), :]
     pl.semaphore_wait(barrier, len(greeted))
 
     column_copies = []
@@ -168,12 +157,12 @@
             copy.start()
             column_copies.append(copy)
 
-    def send_around(ref, which):
+    def send_around(ref, rows, which):
         for a, b, c in around:
             j = (a * 3 + b) * 3 + c
             pltpu.make_async_remote_copy(
-                src_ref=ref.at[pl.ds(home * ROWS, ROWS)],
-                dst_ref=ref.at[pl.ds(j * ROWS, ROWS)],
+                src_ref=ref.at[pl.ds(home * ROWS, rows)],
+                dst_ref=ref.at[pl.ds(j * ROWS, rows)],
                 send_sem=send_sem.at[which],
                 recv_sem=recv_sem.at[which],
                 device_id=peer(1 - a, 1 - b, 1 - c),
@@ -184,17 +173,31 @@
         part = ref.at[pl.ds(0, rows)]
         pltpu.make_async_copy(part, part, sem).wait()
 
-    send_around(speeds, 0)
-    for load in loads[6:]:
+    send_around(speeds, ROWS, 0)
+    for load in loads[5:]:
         load.wait()
-    for copy in column_copies:
-        copy.wait_recv()
-
+
+    lane_row = lax.broadcasted_iota(jnp.int32, (LANES, template), 0)
+    domains = [lax.rem(z + d, nz) for d in range(nz)]
+
+    def lane_factor(domain):
+        member_lane = atoms[domain] & (LANES - 1)
+        for e in range(events):
+            hot = jnp.where(member_lane[e : e + 1] == lane_row, 1.0, 0.0)
+            lanes_hot[domain, :, pl.ds(e * template, template)] = hot.astype(jnp.bfloat16)
+
+    lane_factor(z)
+    for d in range(1, nz):
+        column_copies[2 * d - 1].wait_recv()
+        lane_factor(lax.rem(z - d + nz, nz))
+    for d in range(1, nz):
+        column_copies[2 * d - 2].wait_recv()
+
+    members = jnp.concatenate([atoms[domain] for domain in domains], axis=0)
+    weights = jnp.concatenate([col[domain, pl.ds(ROWS, events), :] for domain in domains], axis=0)
     total_events = nz * events
-    members = atoms[...].reshape(total_events, template)
     member_chunk = lax.shift_right_logical(members, 7)
     member_lane = members & (LANES - 1)
-    weights = jnp.concatenate([col[d, pl.ds(ROWS, events), :] for d in range(nz)], axis=0)
     centred = []
     for i in range(3):
         taken = jnp.zeros((total_events, template), jnp.float32)
@@ -220,29 +223,21 @@
         shifts[3 + i] = shift - coarse
 
     column_chunks = nz * chunks
-    lane_row = lax.broadcasted_iota(jnp.int32, (LANES, template), 0)
     chunk_row = lax.broadcasted_iota(jnp.int32, (column_chunks, template), 0)
     summed = jnp.zeros((6 * column_chunks, LANES), jnp.float32)
-    for first in range(0, total_events, 2):
-        left, right = [], []
-        for e in range(first, first + 2):
-            here = member_chunk[e : e + 1] == chunk_row
-            left.append(
-                jnp.concatenate(
-                    [
-                        jnp.where(here, shifts[q, pl.ds(e, 1), :], 0.0)
-                        for q in range(6)
-                    ],
-                    axis=0,
-                )
+    for d, domain in enumerate(domains):
+        for first in range(0, events, 2):
+            left = []
+            for e in range(d * events + first, d * events + first + 2):
+                here = member_chunk[e : e + 1] == chunk_row
+                parts = [jnp.where(here, shifts[q, pl.ds(e, 1), :], 0.0) for q in range(6)]
+                left.append(jnp.concatenate(parts, axis=0))
+            summed = summed + lax.dot_general(
+                jnp.concatenate(left, axis=1).astype(jnp.bfloat16),
+                lanes_hot[domain, :, pl.ds(first * template, 2 * template)],
+                (((1,), (1,)), ((), ())),
+                preferred_element_type=jnp.float32,
             )
-            right.append(jnp.where(member_lane[e : e + 1] == lane_row, 1.0, 0.0))
-        summed = summed + lax.dot_general(
-            jnp.concatenate(left, axis=1).astype(jnp.bfloat16),
-            jnp.concatenate(right, axis=1).astype(jnp.bfloat16),
-            (((1,), (1,)), ((), ())),
-            preferred_element_type=jnp.float32,
-        )
     half = 3 * column_chunks
     displaced = summed[:half] + summed[half:]
     for d in range(nz):
@@ -256,32 +251,40 @@
     for c in range(3):
         table[pl.ds((home - 1 + c) * ROWS, ROWS), :] = moved[lax.rem(z + c - 1 + nz, nz)]
     for a, b in beside:
-        pltpu.make_async_remote_copy(
-            src_ref=table.at[pl.ds((home - 1) * ROWS, depths * ROWS)],
-            dst_ref=table.at[pl.ds((a * 3 + b) * 3 * ROWS, depths * ROWS)],
-            send_sem=send_sem.at[1],
-            recv_sem=recv_sem.at[1],
-            device_id=peer(1 - a, 1 - b, 0),
-            device_id_type=MESH,
-        ).start()
-    wait_total(table, len(beside) * depths * ROWS, recv_sem.at[1])
+        for c in depth_offsets:
+            pltpu.make_async_remote_copy(
+                src_ref=table.at[pl.ds((home - 1 + c) * ROWS, COORDS)],
+                dst_ref=table.at[pl.ds(((a * 3 + b) * 3 + c) * ROWS, COORDS)],
+                send_sem=send_sem.at[1],
+                recv_sem=recv_sem.at[1],
+                device_id=peer(1 - a, 1 - b, 0),
+                device_id_type=MESH,
+            ).start()
+    wait_total(speeds, len(around) * ROWS, recv_sem.at[0])
+    for a, b, c in around + [(1, 1, 1)]:
+        j = (a * 3 + b) * 3 + c
+        for s in copies(j)[1:]:
+            strengths = pl.ds(s * ROWS + COORDS, ROWS - COORDS)
+            speeds[strengths, :] = speeds[pl.ds(j * ROWS + COORDS, ROWS - COORDS), :]
+    wait_total(table, len(beside) * depths * COORDS, recv_sem.at[1])
     for a, b in beside:
         for c in depth_offsets:
             j = (a * 3 + b) * 3 + c
-            block = table[pl.ds(j * ROWS, ROWS), :]
             for s in copies(j)[1:]:
-                table[pl.ds(s * ROWS, ROWS), :] = block
+                table[pl.ds(s * ROWS, COORDS), :] = table[pl.ds(j * ROWS, COORDS), :]
     for c in range(3):
         j = home - 1 + c
         for s in range(j + 27, slots, 27):
-            table[pl.ds(s * ROWS, ROWS), :] = table[pl.ds(j * ROWS, ROWS), :]
+            table[pl.ds(s * ROWS, COORDS), :] = table[pl.ds(j * ROWS, COORDS), :]
 
     def pair_forces(where, result):
         total = [[jnp.zeros((8, LANES), jnp.float32)] * 3 for _ in range(chunks)]
         for group in range(slots // 8):
             source = [
                 [
-                    where[pl.ds(group * 8 * ROWS + i * chunks + t, 8, stride=ROWS), :]
+                    (where if i < 3 else speeds)[
+                        pl.ds(group * 8 * ROWS + i * chunks + t, 8, stride=ROWS), :
+                    ]
                     for t in range(chunks)
                 ]
                 for i in range(4)
@@ -297,7 +300,8 @@
                         picked = jnp.where(part == t, lane_gather(source[i][t], lane), picked)
                     partner.append(picked)
                 own = [
-                    where[pl.ds(home * ROWS + i * chunks + chunk, 1), :] for i in range(4)
+                    (where if i < 3 else speeds)[pl.ds(home * ROWS + i * chunks + chunk, 1), :]
+                    for i in range(4)
                 ]
                 apart = [own[i] - partner[i] for i in range(3)]
                 square = apart[0] * apart[0] + apart[1] * apart[1] + apart[2] * apart[2]
@@ -314,9 +318,6 @@
                 result[pl.ds(home * ROWS + i * chunks + chunk, 1), :] = jnp.sum(
                     total[chunk][i], axis=0, keepdims=True
                 )
-        result[pl.ds(home * ROWS + 3 * chunks, chunks), :] = jnp.zeros(
-            (chunks, LANES), jnp.float32
-        )
 
     def whole(value):
         return jnp.sum(jnp.sum(value, axis=0, keepdims=True), axis=1, keepdims=True)
@@ -357,21 +358,20 @@
         return keep * (1.0 - mixing), keep * mixing * ratio + time_step
 
     def block(ref, j):
-        return ref[pl.ds(j * ROWS, ROWS), :]
+        return ref[pl.ds(j * ROWS, COORDS), :]
 
     pair_forces(table, forces)
-    send_around(forces, 2)
+    send_around(forces, COORDS, 2)
     sum_start(block(forces, home), block(speeds, home), 0)
-    wait_total(speeds, len(around) * ROWS, recv_sem.at[0])
     old, new = sum_finish(0)
-    wait_total(forces, len(around) * ROWS, recv_sem.at[2])
+    wait_total(forces, len(around) * COORDS, recv_sem.at[2])
     for a, b, c in around + [(1, 1, 1)]:
         j = (a * 3 + b) * 3 + c
         later = block(table, j) + time_step * (
             old * block(speeds, j) + new * block(forces, j)
         )
         for s in copies(j):
-            table2[pl.ds(s * ROWS, ROWS), :] = later
+            table2[pl.ds(s * ROWS, COORDS), :] = later
     speed = old * block(speeds, home) + new * block(forces, home)
 
     pair_forces(table2, forces2)
@@ -390,8 +390,8 @@
     for copy in column_copies:
         copy.wait_send()
     wait_total(speeds, len(around) * ROWS, send_sem.at[0])
-    wait_total(table, len(beside) * depths * ROWS, send_sem.at[1])
-    wait_total(forces, len(around) * ROWS, send_sem.at[2])
+    wait_total(table, len(beside) * depths * COORDS, send_sem.at[1])
+    wait_total(forces, len(around) * COORDS, send_sem.at[2])
     for which in range(2):
         for s, stage in enumerate(stages):
             wait_total(sums, len(stage), sum_send.at[which, s])
@@ -415,12 +415,15 @@
     nx, ny, nz = mesh_shape
     devices = nx * ny * nz
     stages, most = (1, devices) if devices <= DIRECT else (3, max(mesh_shape))
+    alive = jnp.arange(events, dtype=jnp.int32) < event_count.reshape(())
+    live_weights = jnp.where(alive, event_weight.reshape(events), 0.0)
+    live_weights = jnp.broadcast_to(live_weights[:, None], (events, LANES))
     f32, i32 = jnp.float32, jnp.int32
     blocks = pltpu.VMEM((slots * ROWS, LANES), f32)
     outs = pl.pallas_call(
         functools.partial(cycle_kernel, mesh_shape),
         out_shape=[jax.ShapeDtypeStruct((3, 1, atom_count), f32)] * 2,
-        in_specs=[pl.BlockSpec(memory_space=pl.ANY)] * 9,
+        in_specs=[pl.BlockSpec(memory_space=pltpu.HBM)] * 8,
         out_specs=[pl.BlockSpec(memory_space=pltpu.VMEM)] * 2,
         scratch_shapes=[
             pltpu.VMEM((3, 1, atom_count), f32),
@@ -428,20 +431,19 @@
             pltpu.VMEM((1, atom_count), f32),
             pltpu.VMEM((slots, atom_count), i32),
             pltpu.VMEM((slots, atom_count), i32),
-            pltpu.VMEM((1, 1), i32),
             pltpu.VMEM((nz, events, template), i32),
-            pltpu.VMEM((1, events), f32),
             pltpu.VMEM((template, template), f32),
             pltpu.VMEM((nz, ROWS + events, LANES), f32),
             pltpu.VMEM((nz, ROWS, LANES), f32),
             pltpu.VMEM((6, nz * events, template), f32),
+            pltpu.VMEM((nz, LANES, events * template), jnp.bfloat16),
             blocks,
             blocks,
             blocks,
             blocks,
             blocks,
             pltpu.VMEM((2 * stages * most, 1, LANES), f32),
-            pltpu.SemaphoreType.DMA((9,)),
+            pltpu.SemaphoreType.DMA((8,)),
             pltpu.SemaphoreType.DMA((2, 2, nz - 1)),
             pltpu.SemaphoreType.DMA((3,)),
             pltpu.SemaphoreType.DMA((3,)),
@@ -449,7 +451,7 @@
             pltpu.SemaphoreType.DMA((2, stages)),
         ],
         compiler_params=pltpu.CompilerParams(
-            collective_id=0, has_side_effects=True, vmem_limit_bytes=32 * 1024 * 1024
+            collective_id=0, has_side_effects=True, vmem_limit_bytes=60 * 1024 * 1024
         ),
         cost_estimate=pl.CostEstimate(flops=10**7, bytes_accessed=10**6, transcendentals=10**5),
     )(
@@ -458,9 +460,8 @@
         atom_eps.reshape(1, atom_count),
         neighbours.reshape(slots, atom_count),
         pair_live.reshape(slots, atom_count),
-        event_count.reshape(1, 1),
         event_atoms.reshape(events, template),
-        event_weight.reshape(1, events),
+        live_weights,
         template_map,
     )
     return tuple(out.reshape(positions.shape) for out in outs)

time: 33.7 us -> 31.4 us (0.932)
  local copies, waits for them, and re-layouts: 5.08 us -> 3.29 us
  Pallas kernels: 26.9 us -> 26.5 us
    unnamed x18 -> x8, local copies, waits for them, and re-layouts: 5.08 us -> 2.62 us
    broadcast_in_dim x0 -> x1, local copies, waits for them, and re-layouts: none -> 0.67 us  [shards(): live_weights = jnp.broadcast_to(live_weights[:, None], (events, LANES))]
    pallas_call x1, Pallas kernels: 26.9 us -> 26.5 us  [shards(): pl.pallas_call(functools.partial(cycle_kernel, mesh_shape), out_shape=[ja...]
where the time goes in v2:
time: 31.4 us; the launch traced here: 31.1 us
  Pallas kernels  26.5 us (84%)
  local copies, waits for them, and re-layouts  3.29 us (10%)
  between operations  1.3 us (4%)
    pallas_call x1, Pallas kernels, shards(): pl.pallas_call(functools.partial(cycle_kernel, mesh_shape), out_shape=[ja...  26.5 us
    unnamed x8, local copies, waits for them, and re-layouts  2.62 us
    broadcast_in_dim x1, local copies, waits for them, and re-layouts, shards(): live_weights = jnp.broadcast_to(live_weights[:, None], (events, LANES))  0.67 us

profile of v2, /device:TPU:0, one launch (start us, length us, event | category | flops | bytes accessed | tf_op | source)
XLA Modules:
  0.0 31.1 jit_solution(6314230056871826890)
XLA Ops:
  1.3 0.0 copy-start.2
  1.3 0.6 %copy-done.2 = f32[1,1,1,16]{3,2,1,0:T(1,128)S(1)} copy-done((f32[1,1,1,16]{3,2,1,0:T(1,128)S(1)}, f32[1,1,1,16]{3,2,1,0:T(1,128)}, u32[]{:S(2)}) %copy-start.2) | copy-done | bytes 88
  1.9 0.7 %broadcast_in_dim.11.weight_in = f32[16,128]{1,0:T(8,128)} broadcast(f32[16]{0:T(128)S(1)} %compare_select_fusion), dimensions={0} | broadcast | bytes 8256 | tf_op jit(solution)/shard_map/broadcast_in_dim | solution.py:420
  2.6 26.5 %shard_map.104 = (f32[3,1,512]{2,1,0:T(1,128)}, f32[3,1,512]{2,1,0:T(1,128)}) custom-call(f32[3,1,512]{2,1,0:T(1,128)} %bitcast.21, f32[3,1,512]{2,1,0:T(1,128)} %bitcast.22, f32[1,512]{1,0:T(1,128)} %bitcast.23, s32[32,512]{1,0:T(8,128)} %bitcast.16, s32[32,512]{1,0:T(8,128)} %bitcast.17, s32[16,128]{1,0:T(8,128)} %bitcast.18, ...), custom_call_target="tpu_custom_call" | custom-call | flops 10000000 | bytes 1000000 | tf_op jit(solution)/shard_map/pallas_call | solution.py:423
  29.1 0.0 copy-start.1
  29.1 0.7 %copy-done.1 = f32[3,1,512]{2,1,0:T(1,128)S(1)} copy-done((f32[3,1,512]{2,1,0:T(1,128)S(1)}, f32[3,1,512]{2,1,0:T(1,128)}, u32[]{:S(2)}) %copy-start.1) | copy-done | bytes 6168
  29.8 0.0 copy-start
  29.8 0.6 %copy.16 = f32[3,1,1,1,512]{4,3,2,1,0:T(1,128)} copy(f32[3,1,1,1,512]{4,3,2,1,0:T(1,128)S(1)} %bitcast.20) | data formatting | bytes 12288
  30.4 0.1 copy-done
  30.5 0.6 %copy.17 = f32[3,1,1,1,512]{4,3,2,1,0:T(1,128)} copy(f32[3,1,1,1,512]{4,3,2,1,0:T(1,128)S(1)} %bitcast.19) | data formatting | bytes 12288
  (1 shorter events, 0.0 us)
Async XLA Ops:
  1.3 0.7 %copy-start.2 = (f32[1,1,1,16]{3,2,1,0:T(1,128)S(1)}, f32[1,1,1,16]{3,2,1,0:T(1,128)}, u32[]{:S(2)}) copy-start(f32[1,1,1,16]{3,2,1,0:T(1,128)} %param.16) | copy-start | bytes 196
  29.1 0.7 %copy-start.1 = (f32[3,1,512]{2,1,0:T(1,128)S(1)}, f32[3,1,512]{2,1,0:T(1,128)}, u32[]{:S(2)}) copy-start(f32[3,1,512]{2,1,0:T(1,128)} %get-tuple-element.4) | copy-start | bytes 18436
  29.8 0.7 %copy-start = (f32[3,1,512]{2,1,0:T(1,128)S(1)}, f32[3,1,512]{2,1,0:T(1,128)}, u32[]{:S(2)}) copy-start(f32[3,1,512]{2,1,0:T(1,128)} %get-tuple-element.5) | copy-start | bytes 18436

commit v3 on v2

--- a/solution.py
+++ b/solution.py
@@ -16,11 +16,20 @@
 LANES = 128
 COORDS = 12
 ROWS = 16
-DIRECT = 64
+NEAR = 8
 
 
 def lane_gather(table, index):
     return jnp.take_along_axis(table, index, axis=1, mode="promise_in_bounds")
+
+
+def sum_stages(mesh_shape):
+    nx, ny, nz = mesh_shape
+    if nx * nz <= NEAR:
+        first = [[(dx, 0, dz) for dx in range(nx) for dz in range(nz) if (dx, dz) != (0, 0)]]
+    else:
+        first = [[(d, 0, 0) for d in range(1, nx)], [(0, 0, d) for d in range(1, nz)]]
+    return first + [[(0, d, 0) for d in range(1, ny)]]
 
 
 def cycle_kernel(
@@ -30,6 +39,7 @@
     eps_in,
     nbr_in,
     live_in,
+    count_in,
     atoms_in,
     weight_in,
     map_in,
@@ -41,6 +51,7 @@
     nbr,
     live,
     atoms,
+    weight_v,
     tmap,
     col,
     moved,
@@ -60,7 +71,6 @@
     sum_recv,
 ):
     nx, ny, nz = mesh_shape
-    devices = nx * ny * nz
     x, y, z = lax.axis_index("gx"), lax.axis_index("gy"), lax.axis_index("gz")
     slots, atom_count = nbr.shape
     events, template = atoms.shape[1:]
@@ -88,22 +98,7 @@
         if (a, b, c) != (1, 1, 1)
     ]
     beside = [(a, b) for a in range(3) for b in range(3) if (a, b) != (1, 1)]
-    if devices <= DIRECT:
-        stages = [
-            [
-                (dx, dy, dz)
-                for dx in range(nx)
-                for dy in range(ny)
-                for dz in range(nz)
-                if (dx, dy, dz) != (0, 0, 0)
-            ]
-        ]
-    else:
-        stages = [
-            [(d, 0, 0) for d in range(1, nx)],
-            [(0, d, 0) for d in range(1, ny)],
-            [(0, 0, d) for d in range(1, nz)],
-        ]
+    stages = sum_stages(mesh_shape)
     greeted = {((1 - a) % nx, (1 - b) % ny, (1 - c) % nz) for a, b, c in around}
     greeted |= {((a - 1) % nx, (b - 1) % ny, (c - 1) % nz) for a, b, c in around}
     greeted |= {offset for stage in stages for offset in stage}
@@ -115,7 +110,7 @@
         (pos_in, pos_v),
         (vel_in, vel_v),
         (eps_in, eps_v),
-        (weight_in, col.at[z, pl.ds(ROWS, weight_in.shape[0])]),
+        (weight_in, weight_v),
         (atoms_in, own_atoms),
         (map_in, tmap),
         (nbr_in, nbr),
@@ -141,6 +136,14 @@
         row = 3 * chunks + chunk
         col[z, pl.ds(row, 1), :] = jnp.sqrt(eps_v[:, lanes])
         speeds[pl.ds(home * ROWS + row, 1), :] = col[z, pl.ds(row, 1), :]
+    alive = lax.broadcasted_iota(jnp.int32, (1, events), 1) < count_in[0, 0, 0]
+    spread = jnp.broadcast_to(jnp.where(alive, weight_v[...], 0.0), (events, events))
+    diagonal = lax.broadcasted_iota(jnp.int32, (events, events), 0) == lax.broadcasted_iota(
+        jnp.int32, (events, events), 1
+    )
+    column_weight = jnp.sum(jnp.where(diagonal, spread, 0.0), axis=1, keepdims=True)
+    col[z, pl.ds(ROWS, events), :] = jnp.broadcast_to(column_weight, (events, LANES))
+
     pl.semaphore_wait(barrier, len(greeted))
 
     column_copies = []
@@ -248,18 +251,20 @@
         pieces.append(jnp.zeros((chunks, LANES), jnp.float32))
         moved[d] = col[d, pl.ds(0, ROWS), :] + jnp.concatenate(pieces, axis=0)
 
+    def place_of(slot, count=1):
+        return pl.ds(slot * COORDS, count * COORDS)
+
     for c in range(3):
-        table[pl.ds((home - 1 + c) * ROWS, ROWS), :] = moved[lax.rem(z + c - 1 + nz, nz)]
+        table[place_of(home - 1 + c), :] = moved[lax.rem(z + c - 1 + nz, nz), pl.ds(0, COORDS), :]
     for a, b in beside:
-        for c in depth_offsets:
-            pltpu.make_async_remote_copy(
-                src_ref=table.at[pl.ds((home - 1 + c) * ROWS, COORDS)],
-                dst_ref=table.at[pl.ds(((a * 3 + b) * 3 + c) * ROWS, COORDS)],
-                send_sem=send_sem.at[1],
-                recv_sem=recv_sem.at[1],
-                device_id=peer(1 - a, 1 - b, 0),
-                device_id_type=MESH,
-            ).start()
+        pltpu.make_async_remote_copy(
+            src_ref=table.at[place_of(home - 1, depths)],
+            dst_ref=table.at[place_of((a * 3 + b) * 3, depths)],
+            send_sem=send_sem.at[1],
+            recv_sem=recv_sem.at[1],
+            device_id=peer(1 - a, 1 - b, 0),
+            device_id_type=MESH,
+        ).start()
     wait_total(speeds, len(around) * ROWS, recv_sem.at[0])
     for a, b, c in around + [(1, 1, 1)]:
         j = (a * 3 + b) * 3 + c
@@ -271,20 +276,20 @@
         for c in depth_offsets:
             j = (a * 3 + b) * 3 + c
             for s in copies(j)[1:]:
-                table[pl.ds(s * ROWS, COORDS), :] = table[pl.ds(j * ROWS, COORDS), :]
+                table[place_of(s), :] = table[place_of(j), :]
     for c in range(3):
         j = home - 1 + c
         for s in range(j + 27, slots, 27):
-            table[pl.ds(s * ROWS, COORDS), :] = table[pl.ds(j * ROWS, COORDS), :]
+            table[place_of(s), :] = table[place_of(j), :]
 
     def pair_forces(where, result):
         total = [[jnp.zeros((8, LANES), jnp.float32)] * 3 for _ in range(chunks)]
         for group in range(slots // 8):
             source = [
                 [
-                    (where if i < 3 else speeds)[
-                        pl.ds(group * 8 * ROWS + i * chunks + t, 8, stride=ROWS), :
-                    ]
+                    where[pl.ds(group * 8 * COORDS + i * chunks + t, 8, stride=COORDS), :]
+                    if i < 3
+                    else speeds[pl.ds(group * 8 * ROWS + i * chunks + t, 8, stride=ROWS), :]
                     for t in range(chunks)
                 ]
                 for i in range(4)
@@ -300,9 +305,9 @@
                         picked = jnp.where(part == t, lane_gather(source[i][t], lane), picked)
                     partner.append(picked)
                 own = [
-                    (where if i < 3 else speeds)[pl.ds(home * ROWS + i * chunks + chunk, 1), :]
-                    for i in range(4)
+                    where[pl.ds(home * COORDS + i * chunks + chunk, 1), :] for i in range(3)
                 ]
+                own.append(speeds[pl.ds(home * ROWS + COORDS + chunk, 1), :])
                 apart = [own[i] - partner[i] for i in range(3)]
                 square = apart[0] * apart[0] + apart[1] * apart[1] + apart[2] * apart[2]
                 strength = (
@@ -319,17 +324,15 @@
                     total[chunk][i], axis=0, keepdims=True
                 )
 
-    def whole(value):
-        return jnp.sum(jnp.sum(value, axis=0, keepdims=True), axis=1, keepdims=True)
-
-    lane_index = lax.broadcasted_iota(jnp.int32, (1, LANES), 1)
     most = max(len(stage) for stage in stages) + 1
 
+    def fold(value):
+        return jnp.sum(value, axis=0, keepdims=True)
+
     def sum_start(force, speed, which):
-        row = jnp.where(lane_index == 0, whole(force * speed), 0.0)
-        row = jnp.where(lane_index == 1, whole(speed * speed), row)
-        row = jnp.where(lane_index == 2, whole(force * force), row)
-        return stage_start(row, which, 0)
+        rows = [fold(force * speed), fold(speed * speed), fold(force * force)]
+        rows.append(jnp.zeros((5, LANES), jnp.float32))
+        return stage_start(jnp.concatenate(rows, axis=0), which, 0)
 
     def stage_start(row, which, s):
         base = (which * len(stages) + s) * most
@@ -351,7 +354,8 @@
             row = jnp.sum(sums[pl.ds(base, len(stage) + 1)], axis=0)
             if s + 1 < len(stages):
                 stage_start(row, which, s + 1)
-        power, speed_sq, force_sq = row[:, 0:1], row[:, 1:2], row[:, 2:3]
+        total = jnp.sum(row, axis=1, keepdims=True)
+        power, speed_sq, force_sq = total[0:1], total[1:2], total[2:3]
         cosine = power / (jnp.sqrt(speed_sq + epsilon) * jnp.sqrt(force_sq + epsilon))
         ratio = jnp.sqrt((speed_sq + epsilon) / (force_sq + epsilon))
         keep = 0.5 * (1.0 + cosine)
@@ -361,17 +365,17 @@
         return ref[pl.ds(j * ROWS, COORDS), :]
 
     pair_forces(table, forces)
+    sum_start(block(forces, home), block(speeds, home), 0)
     send_around(forces, COORDS, 2)
-    sum_start(block(forces, home), block(speeds, home), 0)
     old, new = sum_finish(0)
     wait_total(forces, len(around) * COORDS, recv_sem.at[2])
     for a, b, c in around + [(1, 1, 1)]:
         j = (a * 3 + b) * 3 + c
-        later = block(table, j) + time_step * (
+        later = table[place_of(j), :] + time_step * (
             old * block(speeds, j) + new * block(forces, j)
         )
         for s in copies(j):
-            table2[pl.ds(s * ROWS, COORDS), :] = later
+            table2[place_of(s), :] = later
     speed = old * block(speeds, home) + new * block(forces, home)
 
     pair_forces(table2, forces2)
@@ -379,13 +383,19 @@
     sum_start(force, speed, 1)
     old, new = sum_finish(1)
     speed = old * speed + new * force
-    place = block(table2, home) + time_step * speed
+    place = table2[place_of(home), :] + time_step * speed
     for chunk in range(chunks):
         lanes = pl.ds(chunk * LANES, LANES)
         for i in range(3):
             row = i * chunks + chunk
-            pos_out[i, :, lanes] = place[row : row + 1]
-            vel_out[i, :, lanes] = speed[row : row + 1]
+            pos_v[i, :, lanes] = place[row : row + 1]
+            vel_v[i, :, lanes] = speed[row : row + 1]
+    stores = [
+        pltpu.make_async_copy(pos_v, pos_out, local_sem.at[0]),
+        pltpu.make_async_copy(vel_v, vel_out, local_sem.at[1]),
+    ]
+    for store in stores:
+        store.start()
 
     for copy in column_copies:
         copy.wait_send()
@@ -395,6 +405,19 @@
     for which in range(2):
         for s, stage in enumerate(stages):
             wait_total(sums, len(stage), sum_send.at[which, s])
+    for store in stores:
+        store.wait()
+
+
+def hand_over(pos, vel, pos_out, vel_out, sem):
+    both = [
+        pltpu.make_async_copy(src, dst, sem.at[i])
+        for i, (src, dst) in enumerate(((pos, pos_out), (vel, vel_out)))
+    ]
+    for copy in both:
+        copy.start()
+    for copy in both:
+        copy.wait()
 
 
 def shards(
@@ -412,19 +435,18 @@
     atom_count = positions.shape[4]
     slots = neighbours.shape[3]
     events, template = event_atoms.shape[3:]
-    nx, ny, nz = mesh_shape
-    devices = nx * ny * nz
-    stages, most = (1, devices) if devices <= DIRECT else (3, max(mesh_shape))
-    alive = jnp.arange(events, dtype=jnp.int32) < event_count.reshape(())
-    live_weights = jnp.where(alive, event_weight.reshape(events), 0.0)
-    live_weights = jnp.broadcast_to(live_weights[:, None], (events, LANES))
+    nz = mesh_shape[2]
+    stages = len(sum_stages(mesh_shape))
+    most = max(len(stage) for stage in sum_stages(mesh_shape)) + 1
     f32, i32 = jnp.float32, jnp.int32
     blocks = pltpu.VMEM((slots * ROWS, LANES), f32)
     outs = pl.pallas_call(
         functools.partial(cycle_kernel, mesh_shape),
         out_shape=[jax.ShapeDtypeStruct((3, 1, atom_count), f32)] * 2,
-        in_specs=[pl.BlockSpec(memory_space=pltpu.HBM)] * 8,
-        out_specs=[pl.BlockSpec(memory_space=pltpu.VMEM)] * 2,
+        in_specs=[pl.BlockSpec(memory_space=pltpu.HBM)] * 5
+        + [pl.BlockSpec(memory_space=pltpu.SMEM)]
+        + [pl.BlockSpec(memory_space=pltpu.HBM)] * 3,
+        out_specs=[pl.BlockSpec(memory_space=pl.ANY)] * 2,
         scratch_shapes=[
             pltpu.VMEM((3, 1, atom_count), f32),
             pltpu.VMEM((3, 1, atom_count), f32),
@@ -432,17 +454,18 @@
             pltpu.VMEM((slots, atom_count), i32),
             pltpu.VMEM((slots, atom_count), i32),
             pltpu.VMEM((nz, events, template), i32),
+            pltpu.VMEM((1, events), f32),
             pltpu.VMEM((template, template), f32),
             pltpu.VMEM((nz, ROWS + events, LANES), f32),
             pltpu.VMEM((nz, ROWS, LANES), f32),
             pltpu.VMEM((6, nz * events, template), f32),
             pltpu.VMEM((nz, LANES, events * template), jnp.bfloat16),
+            pltpu.VMEM((slots * COORDS, LANES), f32),
+            pltpu.VMEM((slots * COORDS, LANES), f32),
             blocks,
             blocks,
             blocks,
-            blocks,
-            blocks,
-            pltpu.VMEM((2 * stages * most, 1, LANES), f32),
+            pltpu.VMEM((2 * stages * most, 8, LANES), f32),
             pltpu.SemaphoreType.DMA((8,)),
             pltpu.SemaphoreType.DMA((2, 2, nz - 1)),
             pltpu.SemaphoreType.DMA((3,)),
@@ -460,11 +483,20 @@
         atom_eps.reshape(1, atom_count),
         neighbours.reshape(slots, atom_count),
         pair_live.reshape(slots, atom_count),
+        event_count,
         event_atoms.reshape(events, template),
-        live_weights,
+        event_weight.reshape(1, events),
         template_map,
     )
-    return tuple(out.reshape(positions.shape) for out in outs)
+    results = pl.pallas_call(
+        hand_over,
+        out_shape=[jax.ShapeDtypeStruct((3, 1, atom_count), f32)] * 2,
+        in_specs=[pl.BlockSpec(memory_space=pl.ANY)] * 2,
+        out_specs=[pl.BlockSpec(memory_space=pl.ANY)] * 2,
+        scratch_shapes=[pltpu.SemaphoreType.DMA((2,))],
+        compiler_params=pltpu.CompilerParams(vmem_limit_bytes=60 * 1024 * 1024),
+    )(*outs)
+    return tuple(result.reshape(positions.shape) for result in results)
 
 
 def solution(mesh):

time: 31.4 us -> 32.1 us (1.022)
  Pallas kernels: 26.5 us -> 30.6 us
  local copies, waits for them, and re-layouts: 3.29 us -> 0 us
    pallas_call x1, Pallas kernels: 26.5 us -> 29.2 us  [shards(): pl.pallas_call(functools.partial(cycle_kernel, mesh_shape), out_shape=[ja...]
    unnamed x8 -> x0, local copies, waits for them, and re-layouts: 2.62 us -> none
    pallas_call x0 -> x1, Pallas kernels: none -> 1.49 us  [shards(): pl.pallas_call(hand_over, out_shape=[jax.ShapeDtypeStruct((3, 1, atom_cou...]
    broadcast_in_dim x1 -> x0, local copies, waits for them, and re-layouts: 0.67 us -> none  [shards(): live_weights = jnp.broadcast_to(live_weights[:, None], (events, LANES))]
where the time goes in v3:
time: 32.1 us; the launch traced here: 31.9 us
  Pallas kernels  30.6 us (95%)
  between operations  1.29 us (4%)
    pallas_call x1, Pallas kernels, shards(): pl.pallas_call(functools.partial(cycle_kernel, mesh_shape), out_shape=[ja...  29.2 us
    pallas_call x1, Pallas kernels, shards(): pl.pallas_call(hand_over, out_shape=[jax.ShapeDtypeStruct((3, 1, atom_cou...  1.49 us

profile of v3, /device:TPU:0, one launch (start us, length us, event | category | flops | bytes accessed | tf_op | source)
XLA Modules:
  0.0 31.9 jit_solution(16120914489401693338)
XLA Ops:
  1.3 29.2 %shard_map.104 = (f32[3,1,512]{2,1,0:T(1,128)}, f32[3,1,512]{2,1,0:T(1,128)}) custom-call(f32[3,1,512]{2,1,0:T(1,128)} %bitcast.16, f32[3,1,512]{2,1,0:T(1,128)} %bitcast.17, f32[1,512]{1,0:T(1,128)} %bitcast.18, s32[32,512]{1,0:T(8,128)} %bitcast.13, s32[32,512]{1,0:T(8,128)} %bitcast.14, s32[1,1,1]{2,1,0:T(1,128)S(6)} %copy.13.count_in, ...), custom_call_target="tpu_custom_call" | custom-call | flops 10000000 | bytes 1000000 | tf_op jit(solution)/shard_map/pallas_call | solution.py:443
  30.4 1.5 %shard_map.105 = (f32[3,1,512]{2,1,0:T(1,128)}, f32[3,1,512]{2,1,0:T(1,128)}) custom-call(f32[3,1,512]{2,1,0:T(1,128)} %get-tuple-element.6.pos, f32[3,1,512]{2,1,0:T(1,128)} %get-tuple-element.7.vel), custom_call_target="tpu_custom_call" | custom-call | tf_op jit(solution)/shard_map/pallas_call | solution.py:491

commit v4 on v3

--- a/solution.py
+++ b/solution.py
@@ -16,7 +16,7 @@
 LANES = 128
 COORDS = 12
 ROWS = 16
-NEAR = 8
+DIRECT = 64
 
 
 def lane_gather(table, index):
@@ -25,11 +25,14 @@
 
 def sum_stages(mesh_shape):
     nx, ny, nz = mesh_shape
-    if nx * nz <= NEAR:
-        first = [[(dx, 0, dz) for dx in range(nx) for dz in range(nz) if (dx, dz) != (0, 0)]]
-    else:
-        first = [[(d, 0, 0) for d in range(1, nx)], [(0, 0, d) for d in range(1, nz)]]
-    return first + [[(0, d, 0) for d in range(1, ny)]]
+    if nx >= 3 and ny >= 3 and nx * ny * nz <= DIRECT:
+        every = [(dx, dy, dz) for dx in range(nx) for dy in range(ny) for dz in range(nz)]
+        return [sorted(every[1:], key=lambda offset: -sum(map(bool, offset)))]
+    return [
+        [(d, 0, 0) for d in range(1, nx)],
+        [(0, 0, d) for d in range(1, nz)],
+        [(0, d, 0) for d in range(1, ny)],
+    ]
 
 
 def cycle_kernel(
@@ -97,13 +100,22 @@
         for c in depth_offsets
         if (a, b, c) != (1, 1, 1)
     ]
+    around.sort(key=lambda direction: -sum(d != 1 for d in direction))
     beside = [(a, b) for a in range(3) for b in range(3) if (a, b) != (1, 1)]
+    beside.sort(key=lambda direction: -sum(d != 1 for d in direction))
     stages = sum_stages(mesh_shape)
+    direct = len(stages) == 1
+    near = {((1 - a) % nx, (1 - b) % ny, (1 - c) % nz) for a, b, c in around}
+    alone = [[offset for offset in stages[0] if offset not in near]] if direct else stages
     greeted = {((1 - a) % nx, (1 - b) % ny, (1 - c) % nz) for a, b, c in around}
     greeted |= {((a - 1) % nx, (b - 1) % ny, (c - 1) % nz) for a, b, c in around}
     greeted |= {offset for stage in stages for offset in stage}
     greeted |= {(0, 0, d) for d in range(1, nz)}
     greeted = sorted(greeted)
+
+    barrier = pltpu.get_barrier_semaphore()
+    for offset in greeted:
+        pl.semaphore_signal(barrier, inc=1, device_id=peer(*offset), device_id_type=MESH)
 
     own_atoms = atoms.at[z]
     pairs = [
@@ -121,9 +133,6 @@
     ]
     for load in loads:
         load.start()
-    barrier = pltpu.get_barrier_semaphore()
-    for offset in greeted:
-        pl.semaphore_signal(barrier, inc=1, device_id=peer(*offset), device_id_type=MESH)
     for load in loads[:5]:
         load.wait()
 
@@ -144,6 +153,16 @@
     column_weight = jnp.sum(jnp.where(diagonal, spread, 0.0), axis=1, keepdims=True)
     col[z, pl.ds(ROWS, events), :] = jnp.broadcast_to(column_weight, (events, LANES))
 
+    lane_row = lax.broadcasted_iota(jnp.int32, (LANES, template), 0)
+    domains = [lax.rem(z + d, nz) for d in range(nz)]
+
+    def lane_factor(domain):
+        member_lane = atoms[domain] & (LANES - 1)
+        for e in range(events):
+            hot = jnp.where(member_lane[e : e + 1] == lane_row, 1.0, 0.0)
+            lanes_hot[domain, :, pl.ds(e * template, template)] = hot.astype(jnp.bfloat16)
+
+    lane_factor(z)
     pl.semaphore_wait(barrier, len(greeted))
 
     column_copies = []
@@ -180,16 +199,6 @@
     for load in loads[5:]:
         load.wait()
 
-    lane_row = lax.broadcasted_iota(jnp.int32, (LANES, template), 0)
-    domains = [lax.rem(z + d, nz) for d in range(nz)]
-
-    def lane_factor(domain):
-        member_lane = atoms[domain] & (LANES - 1)
-        for e in range(events):
-            hot = jnp.where(member_lane[e : e + 1] == lane_row, 1.0, 0.0)
-            lanes_hot[domain, :, pl.ds(e * template, template)] = hot.astype(jnp.bfloat16)
-
-    lane_factor(z)
     for d in range(1, nz):
         column_copies[2 * d - 1].wait_recv()
         lane_factor(lax.rem(z - d + nz, nz))
@@ -329,15 +338,14 @@
     def fold(value):
         return jnp.sum(value, axis=0, keepdims=True)
 
-    def sum_start(force, speed, which):
+    def sum_rows(force, speed):
         rows = [fold(force * speed), fold(speed * speed), fold(force * force)]
-        rows.append(jnp.zeros((5, LANES), jnp.float32))
-        return stage_start(jnp.concatenate(rows, axis=0), which, 0)
+        return jnp.concatenate(rows + [jnp.zeros((1, LANES), jnp.float32)], axis=0)
 
     def stage_start(row, which, s):
         base = (which * len(stages) + s) * most
         sums[base] = row
-        for slot, offset in enumerate(stages[s]):
+        for slot, offset in enumerate((alone, stages)[which][s]):
             pltpu.make_async_remote_copy(
                 src_ref=sums.at[base],
                 dst_ref=sums.at[base + 1 + slot],
@@ -348,12 +356,19 @@
             ).start()
 
     def sum_finish(which):
-        for s, stage in enumerate(stages):
+        for s, stage in enumerate((alone, stages)[which]):
             base = (which * len(stages) + s) * most
-            wait_total(sums, len(stage), sum_recv.at[which, s])
+            if stage:
+                wait_total(sums, len(stage), sum_recv.at[which, s])
             row = jnp.sum(sums[pl.ds(base, len(stage) + 1)], axis=0)
             if s + 1 < len(stages):
                 stage_start(row, which, s + 1)
+        if which == 0:
+            wait_total(forces, len(around) * ROWS, recv_sem.at[2])
+            if direct:
+                for a, b, c in around:
+                    j = (a * 3 + b) * 3 + c
+                    row = row + forces[pl.ds(j * ROWS + COORDS, ROWS - COORDS), :]
         total = jnp.sum(row, axis=1, keepdims=True)
         power, speed_sq, force_sq = total[0:1], total[1:2], total[2:3]
         cosine = power / (jnp.sqrt(speed_sq + epsilon) * jnp.sqrt(force_sq + epsilon))
@@ -365,10 +380,11 @@
         return ref[pl.ds(j * ROWS, COORDS), :]
 
     pair_forces(table, forces)
-    sum_start(block(forces, home), block(speeds, home), 0)
-    send_around(forces, COORDS, 2)
+    row = sum_rows(block(forces, home), block(speeds, home))
+    forces[pl.ds(home * ROWS + COORDS, ROWS - COORDS), :] = row
+    send_around(forces, ROWS, 2)
+    stage_start(row, 0, 0)
     old, new = sum_finish(0)
-    wait_total(forces, len(around) * COORDS, recv_sem.at[2])
     for a, b, c in around + [(1, 1, 1)]:
         j = (a * 3 + b) * 3 + c
         later = table[place_of(j), :] + time_step * (
@@ -380,7 +396,7 @@
 
     pair_forces(table2, forces2)
     force = block(forces2, home)
-    sum_start(force, speed, 1)
+    stage_start(sum_rows(force, speed), 1, 0)
     old, new = sum_finish(1)
     speed = old * speed + new * force
     place = table2[place_of(home), :] + time_step * speed
@@ -401,10 +417,11 @@
         copy.wait_send()
     wait_total(speeds, len(around) * ROWS, send_sem.at[0])
     wait_total(table, len(beside) * depths * COORDS, send_sem.at[1])
-    wait_total(forces, len(around) * COORDS, send_sem.at[2])
+    wait_total(forces, len(around) * ROWS, send_sem.at[2])
     for which in range(2):
-        for s, stage in enumerate(stages):
-            wait_total(sums, len(stage), sum_send.at[which, s])
+        for s, stage in enumerate((alone, stages)[which]):
+            if stage:
+                wait_total(sums, len(stage), sum_send.at[which, s])
     for store in stores:
         store.wait()
 
@@ -465,7 +482,7 @@
             blocks,
             blocks,
             blocks,
-            pltpu.VMEM((2 * stages * most, 8, LANES), f32),
+            pltpu.VMEM((2 * stages * most, 4, LANES), f32),
             pltpu.SemaphoreType.DMA((8,)),
             pltpu.SemaphoreType.DMA((2, 2, nz - 1)),
             pltpu.SemaphoreType.DMA((3,)),

time: 32.1 us -> 30.4 us (0.947)
  Pallas kernels: 30.6 us -> 28.9 us
    pallas_call x1, Pallas kernels: 29.2 us -> 27.4 us  [shards(): pl.pallas_call(functools.partial(cycle_kernel, mesh_shape), out_shape=[ja...]
where the time goes in v4:
time: 30.4 us; the launch traced here: 30.2 us
  Pallas kernels  28.9 us (95%)
  between operations  1.29 us (4%)
    pallas_call x1, Pallas kernels, shards(): pl.pallas_call(functools.partial(cycle_kernel, mesh_shape), out_shape=[ja...  27.4 us
    pallas_call x1, Pallas kernels, shards(): pl.pallas_call(hand_over, out_shape=[jax.ShapeDtypeStruct((3, 1, atom_cou...  1.49 us

profile of v4, /device:TPU:0, one launch (start us, length us, event | category | flops | bytes accessed | tf_op | source)
XLA Modules:
  0.0 30.2 jit_solution(1352110991834340736)
XLA Ops:
  1.3 27.4 %shard_map.104 = (f32[3,1,512]{2,1,0:T(1,128)}, f32[3,1,512]{2,1,0:T(1,128)}) custom-call(f32[3,1,512]{2,1,0:T(1,128)} %bitcast.16, f32[3,1,512]{2,1,0:T(1,128)} %bitcast.17, f32[1,512]{1,0:T(1,128)} %bitcast.18, s32[32,512]{1,0:T(8,128)} %bitcast.13, s32[32,512]{1,0:T(8,128)} %bitcast.14, s32[1,1,1]{2,1,0:T(1,128)S(6)} %copy.13.count_in, ...), custom_call_target="tpu_custom_call" | custom-call | flops 10000000 | bytes 1000000 | tf_op jit(solution)/shard_map/pallas_call | solution.py:460
  28.7 1.5 %shard_map.105 = (f32[3,1,512]{2,1,0:T(1,128)}, f32[3,1,512]{2,1,0:T(1,128)}) custom-call(f32[3,1,512]{2,1,0:T(1,128)} %get-tuple-element.6.pos, f32[3,1,512]{2,1,0:T(1,128)} %get-tuple-element.7.vel), custom_call_target="tpu_custom_call" | custom-call | tf_op jit(solution)/shard_map/pallas_call | solution.py:508

commit v5 on v4

--- a/solution.py
+++ b/solution.py
@@ -162,7 +162,6 @@
             hot = jnp.where(member_lane[e : e + 1] == lane_row, 1.0, 0.0)
             lanes_hot[domain, :, pl.ds(e * template, template)] = hot.astype(jnp.bfloat16)
 
-    lane_factor(z)
     pl.semaphore_wait(barrier, len(greeted))
 
     column_copies = []
@@ -199,6 +198,7 @@
     for load in loads[5:]:
         load.wait()
 
+    lane_factor(z)
     for d in range(1, nz):
         column_copies[2 * d - 1].wait_recv()
         lane_factor(lax.rem(z - d + nz, nz))
@@ -260,20 +260,21 @@
         pieces.append(jnp.zeros((chunks, LANES), jnp.float32))
         moved[d] = col[d, pl.ds(0, ROWS), :] + jnp.concatenate(pieces, axis=0)
 
-    def place_of(slot, count=1):
-        return pl.ds(slot * COORDS, count * COORDS)
+    def place_of(slot):
+        return pl.ds(slot * ROWS, COORDS)
 
     for c in range(3):
         table[place_of(home - 1 + c), :] = moved[lax.rem(z + c - 1 + nz, nz), pl.ds(0, COORDS), :]
     for a, b in beside:
-        pltpu.make_async_remote_copy(
-            src_ref=table.at[place_of(home - 1, depths)],
-            dst_ref=table.at[place_of((a * 3 + b) * 3, depths)],
-            send_sem=send_sem.at[1],
-            recv_sem=recv_sem.at[1],
-            device_id=peer(1 - a, 1 - b, 0),
-            device_id_type=MESH,
-        ).start()
+        for c in depth_offsets:
+            pltpu.make_async_remote_copy(
+                src_ref=table.at[place_of(home - 1 + c)],
+                dst_ref=table.at[place_of((a * 3 + b) * 3 + c)],
+                send_sem=send_sem.at[1],
+                recv_sem=recv_sem.at[1],
+                device_id=peer(1 - a, 1 - b, 0),
+                device_id_type=MESH,
+            ).start()
     wait_total(speeds, len(around) * ROWS, recv_sem.at[0])
     for a, b, c in around + [(1, 1, 1)]:
         j = (a * 3 + b) * 3 + c
@@ -296,9 +297,9 @@
         for group in range(slots // 8):
             source = [
                 [
-                    where[pl.ds(group * 8 * COORDS + i * chunks + t, 8, stride=COORDS), :]
-                    if i < 3
-                    else speeds[pl.ds(group * 8 * ROWS + i * chunks + t, 8, stride=ROWS), :]
+                    (where if i < 3 else speeds)[
+                        pl.ds(group * 8 * ROWS + i * chunks + t, 8, stride=ROWS), :
+                    ]
                     for t in range(chunks)
                 ]
                 for i in range(4)
@@ -314,7 +315,7 @@
                         picked = jnp.where(part == t, lane_gather(source[i][t], lane), picked)
                     partner.append(picked)
                 own = [
-                    where[pl.ds(home * COORDS + i * chunks + chunk, 1), :] for i in range(3)
+                    where[pl.ds(home * ROWS + i * chunks + chunk, 1), :] for i in range(3)
                 ]
                 own.append(speeds[pl.ds(home * ROWS + COORDS + chunk, 1), :])
                 apart = [own[i] - partner[i] for i in range(3)]
@@ -338,9 +339,13 @@
     def fold(value):
         return jnp.sum(value, axis=0, keepdims=True)
 
-    def sum_rows(force, speed):
-        rows = [fold(force * speed), fold(speed * speed), fold(force * force)]
-        return jnp.concatenate(rows + [jnp.zeros((1, LANES), jnp.float32)], axis=0)
+    lane_index = lax.broadcasted_iota(jnp.int32, (1, LANES), 1)
+
+    def sum_row(force, speed):
+        parts = [fold(force * speed), fold(speed * speed), fold(force * force)]
+        power, speed_sq, force_sq = [jnp.sum(part, axis=1, keepdims=True) for part in parts]
+        row = jnp.where(lane_index == 0, power, jnp.where(lane_index == 1, speed_sq, 0.0))
+        return jnp.where(lane_index == 2, force_sq, row)
 
     def stage_start(row, which, s):
         base = (which * len(stages) + s) * most
@@ -364,13 +369,12 @@
             if s + 1 < len(stages):
                 stage_start(row, which, s + 1)
         if which == 0:
-            wait_total(forces, len(around) * ROWS, recv_sem.at[2])
+            wait_total(forces, len(around) * (COORDS + 1), recv_sem.at[2])
             if direct:
                 for a, b, c in around:
                     j = (a * 3 + b) * 3 + c
-                    row = row + forces[pl.ds(j * ROWS + COORDS, ROWS - COORDS), :]
-        total = jnp.sum(row, axis=1, keepdims=True)
-        power, speed_sq, force_sq = total[0:1], total[1:2], total[2:3]
+                    row = row + forces[pl.ds(j * ROWS + COORDS, 1), :]
+        power, speed_sq, force_sq = row[:, 0:1], row[:, 1:2], row[:, 2:3]
         cosine = power / (jnp.sqrt(speed_sq + epsilon) * jnp.sqrt(force_sq + epsilon))
         ratio = jnp.sqrt((speed_sq + epsilon) / (force_sq + epsilon))
         keep = 0.5 * (1.0 + cosine)
@@ -380,9 +384,9 @@
         return ref[pl.ds(j * ROWS, COORDS), :]
 
     pair_forces(table, forces)
-    row = sum_rows(block(forces, home), block(speeds, home))
-    forces[pl.ds(home * ROWS + COORDS, ROWS - COORDS), :] = row
-    send_around(forces, ROWS, 2)
+    row = sum_row(block(forces, home), block(speeds, home))
+    forces[pl.ds(home * ROWS + COORDS, 1), :] = row
+    send_around(forces, COORDS + 1, 2)
     stage_start(row, 0, 0)
     old, new = sum_finish(0)
     for a, b, c in around + [(1, 1, 1)]:
@@ -396,7 +400,7 @@
 
     pair_forces(table2, forces2)
     force = block(forces2, home)
-    stage_start(sum_rows(force, speed), 1, 0)
+    stage_start(sum_row(force, speed), 1, 0)
     old, new = sum_finish(1)
     speed = old * speed + new * force
     place = table2[place_of(home), :] + time_step * speed
@@ -404,37 +408,17 @@
         lanes = pl.ds(chunk * LANES, LANES)
         for i in range(3):
             row = i * chunks + chunk
-            pos_v[i, :, lanes] = place[row : row + 1]
-            vel_v[i, :, lanes] = speed[row : row + 1]
-    stores = [
-        pltpu.make_async_copy(pos_v, pos_out, local_sem.at[0]),
-        pltpu.make_async_copy(vel_v, vel_out, local_sem.at[1]),
-    ]
-    for store in stores:
-        store.start()
-
+            pos_out[i, :, lanes] = place[row : row + 1]
+            vel_out[i, :, lanes] = speed[row : row + 1]
     for copy in column_copies:
         copy.wait_send()
     wait_total(speeds, len(around) * ROWS, send_sem.at[0])
     wait_total(table, len(beside) * depths * COORDS, send_sem.at[1])
-    wait_total(forces, len(around) * ROWS, send_sem.at[2])
+    wait_total(forces, len(around) * (COORDS + 1), send_sem.at[2])
     for which in range(2):
         for s, stage in enumerate((alone, stages)[which]):
             if stage:
                 wait_total(sums, len(stage), sum_send.at[which, s])
-    for store in stores:
-        store.wait()
-
-
-def hand_over(pos, vel, pos_out, vel_out, sem):
-    both = [
-        pltpu.make_async_copy(src, dst, sem.at[i])
-        for i, (src, dst) in enumerate(((pos, pos_out), (vel, vel_out)))
-    ]
-    for copy in both:
-        copy.start()
-    for copy in both:
-        copy.wait()
 
 
 def shards(
@@ -463,7 +447,7 @@
         in_specs=[pl.BlockSpec(memory_space=pltpu.HBM)] * 5
         + [pl.BlockSpec(memory_space=pltpu.SMEM)]
         + [pl.BlockSpec(memory_space=pltpu.HBM)] * 3,
-        out_specs=[pl.BlockSpec(memory_space=pl.ANY)] * 2,
+        out_specs=[pl.BlockSpec(memory_space=pltpu.VMEM)] * 2,
         scratch_shapes=[
             pltpu.VMEM((3, 1, atom_count), f32),
             pltpu.VMEM((3, 1, atom_count), f32),
@@ -477,12 +461,12 @@
             pltpu.VMEM((nz, ROWS, LANES), f32),
             pltpu.VMEM((6, nz * events, template), f32),
             pltpu.VMEM((nz, LANES, events * template), jnp.bfloat16),
-            pltpu.VMEM((slots * COORDS, LANES), f32),
-            pltpu.VMEM((slots * COORDS, LANES), f32),
             blocks,
             blocks,
             blocks,
-            pltpu.VMEM((2 * stages * most, 4, LANES), f32),
+            blocks,
+            blocks,
+            pltpu.VMEM((2 * stages * most, 1, LANES), f32),
             pltpu.SemaphoreType.DMA((8,)),
             pltpu.SemaphoreType.DMA((2, 2, nz - 1)),
             pltpu.SemaphoreType.DMA((3,)),
@@ -491,7 +475,7 @@
             pltpu.SemaphoreType.DMA((2, stages)),
         ],
         compiler_params=pltpu.CompilerParams(
-            collective_id=0, has_side_effects=True, vmem_limit_bytes=60 * 1024 * 1024
+            collective_id=0, has_side_effects=True, vmem_limit_bytes=56520704
         ),
         cost_estimate=pl.CostEstimate(flops=10**7, bytes_accessed=10**6, transcendentals=10**5),
     )(
@@ -505,15 +489,7 @@
         event_weight.reshape(1, events),
         template_map,
     )
-    results = pl.pallas_call(
-        hand_over,
-        out_shape=[jax.ShapeDtypeStruct((3, 1, atom_count), f32)] * 2,
-        in_specs=[pl.BlockSpec(memory_space=pl.ANY)] * 2,
-        out_specs=[pl.BlockSpec(memory_space=pl.ANY)] * 2,
-        scratch_shapes=[pltpu.SemaphoreType.DMA((2,))],
-        compiler_params=pltpu.CompilerParams(vmem_limit_bytes=60 * 1024 * 1024),
-    )(*outs)
-    return tuple(result.reshape(positions.shape) for result in results)
+    return tuple(result.reshape(positions.shape) for result in outs)
 
 
 def solution(mesh):

time: 30.4 us -> 29.4 us (0.967)
  Pallas kernels: 28.9 us -> 25.9 us
  local copies, waits for them, and re-layouts: 0 us -> 1.86 us
    unnamed x0 -> x8, local copies, waits for them, and re-layouts: none -> 1.86 us
    pallas_call x1, Pallas kernels: 27.4 us -> 25.9 us  [shards(): pl.pallas_call(functools.partial(cycle_kernel, mesh_shape), out_shape=[ja...]
    pallas_call x1 -> x0, Pallas kernels: 1.49 us -> none  [shards(): pl.pallas_call(hand_over, out_shape=[jax.ShapeDtypeStruct((3, 1, atom_cou...]
where the time goes in v5:
time: 29.4 us; the launch traced here: 29.1 us
  Pallas kernels  25.9 us (88%)
  local copies, waits for them, and re-layouts  1.86 us (6%)
  between operations  1.31 us (4%)
    pallas_call x1, Pallas kernels, shards(): pl.pallas_call(functools.partial(cycle_kernel, mesh_shape), out_shape=[ja...  25.9 us
    unnamed x8, local copies, waits for them, and re-layouts  1.86 us

profile of v5, /device:TPU:0, one launch (start us, length us, event | category | flops | bytes accessed | tf_op | source)
XLA Modules:
  0.0 29.1 jit_solution(8845594383534578405)
XLA Ops:
  1.3 0.0 copy-start
  1.3 0.0 copy-start.1
  1.3 0.0 copy-start.2
  1.3 0.7 %copy-done = f32[3,1,1,1,512]{4,3,2,1,0:T(1,128)S(1)} copy-done((f32[3,1,1,1,512]{4,3,2,1,0:T(1,128)S(1)}, f32[3,1,1,1,512]{4,3,2,1,0:T(1,128)}, u32[]{:S(2)}) %copy-start) | copy-done | bytes 6168
  2.0 0.0 copy-done.1
  2.0 0.0 copy-done.2
  2.0 25.9 %shard_map.104 = (f32[3,1,512]{2,1,0:T(1,128)S(1)}, f32[3,1,512]{2,1,0:T(1,128)S(1)}) custom-call(f32[3,1,512]{2,1,0:T(1,128)S(1)} %bitcast.13, f32[3,1,512]{2,1,0:T(1,128)} %bitcast.21, f32[1,512]{1,0:T(1,128)S(1)} %bitcast.16, s32[32,512]{1,0:T(8,128)} %bitcast.18, s32[32,512]{1,0:T(8,128)} %bitcast.19, s32[1,1,1]{2,1,0:T(1,128)S(6)} %copy.15.count_in, ...), custom_call_target="tpu_custom_call" | custom-call | flops 10000000 | bytes 1000000 | tf_op jit(solution)/shard_map/pallas_call | solution.py:444
  27.9 0.6 %copy.16 = f32[3,1,1,1,512]{4,3,2,1,0:T(1,128)} copy(f32[3,1,1,1,512]{4,3,2,1,0:T(1,128)S(1)} %bitcast.15) | data formatting | bytes 12288
  28.5 0.6 %copy.17 = f32[3,1,1,1,512]{4,3,2,1,0:T(1,128)} copy(f32[3,1,1,1,512]{4,3,2,1,0:T(1,128)S(1)} %bitcast.14) | data formatting | bytes 12288
Async XLA Ops:
  1.3 0.7 %copy-start = (f32[3,1,1,1,512]{4,3,2,1,0:T(1,128)S(1)}, f32[3,1,1,1,512]{4,3,2,1,0:T(1,128)}, u32[]{:S(2)}) copy-start(f32[3,1,1,1,512]{4,3,2,1,0:T(1,128)} %param.9) | copy-start | bytes 18436
  1.3 0.7 %copy-start.1 = (f32[1,1,1,512]{3,2,1,0:T(1,128)S(1)}, f32[1,1,1,512]{3,2,1,0:T(1,128)}, u32[]{:S(2)}) copy-start(f32[1,1,1,512]{3,2,1,0:T(1,128)} %param.11) | copy-start | bytes 6148
  1.3 0.7 %copy-start.2 = (f32[1,1,1,16]{3,2,1,0:T(1,128)S(1)}, f32[1,1,1,16]{3,2,1,0:T(1,128)}, u32[]{:S(2)}) copy-start(f32[1,1,1,16]{3,2,1,0:T(1,128)} %param.16) | copy-start | bytes 196

commit v6 on v5

--- a/solution.py
+++ b/solution.py
@@ -60,6 +60,7 @@
     moved,
     shifts,
     lanes_hot,
+    factor,
     table,
     table2,
     speeds,
@@ -199,11 +200,10 @@
         load.wait()
 
     lane_factor(z)
+    for copy in column_copies:
+        copy.wait_recv()
     for d in range(1, nz):
-        column_copies[2 * d - 1].wait_recv()
         lane_factor(lax.rem(z - d + nz, nz))
-    for d in range(1, nz):
-        column_copies[2 * d - 2].wait_recv()
 
     members = jnp.concatenate([atoms[domain] for domain in domains], axis=0)
     weights = jnp.concatenate([col[domain, pl.ds(ROWS, events), :] for domain in domains], axis=0)
@@ -281,6 +281,29 @@
         for s in copies(j)[1:]:
             strengths = pl.ds(s * ROWS + COORDS, ROWS - COORDS)
             speeds[strengths, :] = speeds[pl.ds(j * ROWS + COORDS, ROWS - COORDS), :]
+
+    def pick(source, index):
+        lane, part = index & (LANES - 1), lax.shift_right_logical(index, 7)
+        picked = lane_gather(source[0], lane)
+        for t in range(1, chunks):
+            picked = jnp.where(part == t, lane_gather(source[t], lane), picked)
+        return picked
+
+    for group in range(slots // 8):
+        rows = pl.ds(group * 8, 8)
+        source = [
+            speeds[pl.ds(group * 8 * ROWS + COORDS + t, 8, stride=ROWS), :] for t in range(chunks)
+        ]
+        for chunk in range(chunks):
+            lanes = pl.ds(chunk * LANES, LANES)
+            own = speeds[pl.ds(home * ROWS + COORDS + chunk, 1), :]
+            factor[rows, lanes] = (
+                own
+                * pick(source, nbr[rows, lanes])
+                * live[rows, lanes].astype(jnp.float32)
+                * (1.0 / (width_scale * width_scale))
+            )
+
     wait_total(table, len(beside) * depths * COORDS, recv_sem.at[1])
     for a, b in beside:
         for c in depth_offsets:
@@ -297,35 +320,21 @@
         for group in range(slots // 8):
             source = [
                 [
-                    (where if i < 3 else speeds)[
-                        pl.ds(group * 8 * ROWS + i * chunks + t, 8, stride=ROWS), :
-                    ]
+                    where[pl.ds(group * 8 * ROWS + i * chunks + t, 8, stride=ROWS), :]
                     for t in range(chunks)
                 ]
-                for i in range(4)
+                for i in range(3)
             ]
             for chunk in range(chunks):
                 rows, lanes = pl.ds(group * 8, 8), pl.ds(chunk * LANES, LANES)
                 index = nbr[rows, lanes]
-                lane, part = index & (LANES - 1), lax.shift_right_logical(index, 7)
-                partner = []
-                for i in range(4):
-                    picked = lane_gather(source[i][0], lane)
-                    for t in range(1, chunks):
-                        picked = jnp.where(part == t, lane_gather(source[i][t], lane), picked)
-                    partner.append(picked)
-                own = [
-                    where[pl.ds(home * ROWS + i * chunks + chunk, 1), :] for i in range(3)
+                apart = [
+                    where[pl.ds(home * ROWS + i * chunks + chunk, 1), :] - pick(source[i], index)
+                    for i in range(3)
                 ]
-                own.append(speeds[pl.ds(home * ROWS + COORDS + chunk, 1), :])
-                apart = [own[i] - partner[i] for i in range(3)]
                 square = apart[0] * apart[0] + apart[1] * apart[1] + apart[2] * apart[2]
-                strength = (
-                    own[3]
-                    * partner[3]
-                    * live[rows, lanes].astype(jnp.float32)
-                    * jnp.exp(square * (-0.5 / (width_scale * width_scale)))
-                    * (1.0 / (width_scale * width_scale))
+                strength = factor[rows, lanes] * jnp.exp(
+                    square * (-0.5 / (width_scale * width_scale))
                 )
                 total[chunk] = [total[chunk][i] + strength * apart[i] for i in range(3)]
         for chunk in range(chunks):
@@ -461,6 +470,7 @@
             pltpu.VMEM((nz, ROWS, LANES), f32),
             pltpu.VMEM((6, nz * events, template), f32),
             pltpu.VMEM((nz, LANES, events * template), jnp.bfloat16),
+            pltpu.VMEM((slots, atom_count), f32),
             blocks,
             blocks,
             blocks,

time: 29.4 us -> 29.1 us (0.990)
  no operation moved by 1% of the time
where the time goes in v6:
time: 29.1 us; the launch traced here: 28.9 us
  Pallas kernels  25.7 us (88%)
  local copies, waits for them, and re-layouts  1.86 us (6%)
  between operations  1.31 us (5%)
    pallas_call x1, Pallas kernels, shards(): pl.pallas_call(functools.partial(cycle_kernel, mesh_shape), out_shape=[ja...  25.7 us
    unnamed x8, local copies, waits for them, and re-layouts  1.86 us

profile of v6, /device:TPU:0, one launch (start us, length us, event | category | flops | bytes accessed | tf_op | source)
XLA Modules:
  0.0 28.9 jit_solution(1867874406959486351)
XLA Ops:
  1.3 0.0 copy-start
  1.3 0.0 copy-start.1
  1.3 0.0 copy-start.2
  1.3 0.7 %copy-done = f32[3,1,1,1,512]{4,3,2,1,0:T(1,128)S(1)} copy-done((f32[3,1,1,1,512]{4,3,2,1,0:T(1,128)S(1)}, f32[3,1,1,1,512]{4,3,2,1,0:T(1,128)}, u32[]{:S(2)}) %copy-start) | copy-done | bytes 6168
  2.0 0.0 copy-done.1
  2.0 0.0 copy-done.2
  2.0 25.7 %shard_map.104 = (f32[3,1,512]{2,1,0:T(1,128)S(1)}, f32[3,1,512]{2,1,0:T(1,128)S(1)}) custom-call(f32[3,1,512]{2,1,0:T(1,128)S(1)} %bitcast.13, f32[3,1,512]{2,1,0:T(1,128)} %bitcast.21, f32[1,512]{1,0:T(1,128)S(1)} %bitcast.16, s32[32,512]{1,0:T(8,128)} %bitcast.18, s32[32,512]{1,0:T(8,128)} %bitcast.19, s32[1,1,1]{2,1,0:T(1,128)S(6)} %copy.15.count_in, ...), custom_call_target="tpu_custom_call" | custom-call | flops 10000000 | bytes 1000000 | tf_op jit(solution)/shard_map/pallas_call | solution.py:453
  27.7 0.6 %copy.16 = f32[3,1,1,1,512]{4,3,2,1,0:T(1,128)} copy(f32[3,1,1,1,512]{4,3,2,1,0:T(1,128)S(1)} %bitcast.15) | data formatting | bytes 12288
  28.3 0.6 %copy.17 = f32[3,1,1,1,512]{4,3,2,1,0:T(1,128)} copy(f32[3,1,1,1,512]{4,3,2,1,0:T(1,128)S(1)} %bitcast.14) | data formatting | bytes 12288
Async XLA Ops:
  1.3 0.7 %copy-start = (f32[3,1,1,1,512]{4,3,2,1,0:T(1,128)S(1)}, f32[3,1,1,1,512]{4,3,2,1,0:T(1,128)}, u32[]{:S(2)}) copy-start(f32[3,1,1,1,512]{4,3,2,1,0:T(1,128)} %param.9) | copy-start | bytes 18436
  1.3 0.7 %copy-start.1 = (f32[1,1,1,512]{3,2,1,0:T(1,128)S(1)}, f32[1,1,1,512]{3,2,1,0:T(1,128)}, u32[]{:S(2)}) copy-start(f32[1,1,1,512]{3,2,1,0:T(1,128)} %param.11) | copy-start | bytes 6148
  1.3 0.7 %copy-start.2 = (f32[1,1,1,16]{3,2,1,0:T(1,128)S(1)}, f32[1,1,1,16]{3,2,1,0:T(1,128)}, u32[]{:S(2)}) copy-start(f32[1,1,1,16]{3,2,1,0:T(1,128)} %param.16) | copy-start | bytes 196

commit v7 on v6

--- a/solution.py
+++ b/solution.py
@@ -428,6 +428,17 @@
         for s, stage in enumerate((alone, stages)[which]):
             if stage:
                 wait_total(sums, len(stage), sum_send.at[which, s])
+
+
+def hand_over(pos, vel, pos_out, vel_out, sem):
+    both = [
+        pltpu.make_async_copy(src, dst, sem.at[i])
+        for i, (src, dst) in enumerate(((pos, pos_out), (vel, vel_out)))
+    ]
+    for copy in both:
+        copy.start()
+    for copy in both:
+        copy.wait()
 
 
 def shards(
@@ -499,7 +510,14 @@
         event_weight.reshape(1, events),
         template_map,
     )
-    return tuple(result.reshape(positions.shape) for result in outs)
+    results = pl.pallas_call(
+        hand_over,
+        out_shape=[jax.ShapeDtypeStruct((3, 1, atom_count), f32)] * 2,
+        in_specs=[pl.BlockSpec(memory_space=pl.ANY)] * 2,
+        out_specs=[pl.BlockSpec(memory_space=pl.ANY)] * 2,
+        scratch_shapes=[pltpu.SemaphoreType.DMA((2,))],
+    )(*outs)
+    return tuple(result.reshape(positions.shape) for result in results)
 
 
 def solution(mesh):

time: 29.1 us -> 30.6 us (1.052)
  Pallas kernels: 25.7 us -> 27.2 us
    pallas_call x0 -> x1, Pallas kernels: none -> 1.49 us  [shards(): pl.pallas_call(hand_over, out_shape=[jax.ShapeDtypeStruct((3, 1, atom_cou...]
    unnamed x8 -> x10, local copies, waits for them, and re-layouts: 1.86 us -> 1.86 us
where the time goes in v7:
time: 30.6 us; the launch traced here: 30.4 us
  Pallas kernels  27.2 us (89%)
  local copies, waits for them, and re-layouts  1.86 us (6%)
  between operations  1.32 us (4%)
    pallas_call x1, Pallas kernels, shards(): pl.pallas_call(functools.partial(cycle_kernel, mesh_shape), out_shape=[ja...  25.7 us
    unnamed x10, local copies, waits for them, and re-layouts  1.86 us
    pallas_call x1, Pallas kernels, shards(): pl.pallas_call(hand_over, out_shape=[jax.ShapeDtypeStruct((3, 1, atom_cou...  1.49 us

profile of v7, /device:TPU:0, one launch (start us, length us, event | category | flops | bytes accessed | tf_op | source)
XLA Modules:
  0.0 30.4 jit_solution(5285734123644912284)
XLA Ops:
  1.3 0.0 copy-start
  1.3 0.0 copy-start.3
  1.3 0.0 copy-start.4
  1.3 0.7 %copy-done = f32[3,1,1,1,512]{4,3,2,1,0:T(1,128)S(1)} copy-done((f32[3,1,1,1,512]{4,3,2,1,0:T(1,128)S(1)}, f32[3,1,1,1,512]{4,3,2,1,0:T(1,128)}, u32[]{:S(2)}) %copy-start) | copy-done | bytes 6168
  2.0 0.0 copy-done.3
  2.0 0.0 copy-done.4
  2.0 25.7 %shard_map.104 = (f32[3,1,512]{2,1,0:T(1,128)S(1)}, f32[3,1,512]{2,1,0:T(1,128)S(1)}) custom-call(f32[3,1,512]{2,1,0:T(1,128)S(1)} %bitcast.13, f32[3,1,512]{2,1,0:T(1,128)} %bitcast.19, f32[1,512]{1,0:T(1,128)S(1)} %bitcast.14, s32[32,512]{1,0:T(8,128)} %bitcast.16, s32[32,512]{1,0:T(8,128)} %bitcast.17, s32[1,1,1]{2,1,0:T(1,128)S(6)} %copy.13.count_in, ...), custom_call_target="tpu_custom_call" | custom-call | flops 10000000 | bytes 1000000 | tf_op jit(solution)/shard_map/pallas_call | solution.py:464
  27.7 0.0 copy-start.1
  27.7 0.6 %copy-done.1 = f32[3,1,512]{2,1,0:T(1,128)} copy-done((f32[3,1,512]{2,1,0:T(1,128)}, f32[3,1,512]{2,1,0:T(1,128)S(1)}, u32[]{:S(2)}) %copy-start.1) | copy-done | bytes 6168
  28.3 0.0 copy-start.2
  28.3 0.6 %copy-done.2 = f32[3,1,512]{2,1,0:T(1,128)} copy-done((f32[3,1,512]{2,1,0:T(1,128)}, f32[3,1,512]{2,1,0:T(1,128)S(1)}, u32[]{:S(2)}) %copy-start.2) | copy-done | bytes 6168
  28.9 1.5 %shard_map.105 = (f32[3,1,512]{2,1,0:T(1,128)}, f32[3,1,512]{2,1,0:T(1,128)}) custom-call(f32[3,1,512]{2,1,0:T(1,128)} %copy-done.1, f32[3,1,512]{2,1,0:T(1,128)} %copy-done.2), custom_call_target="tpu_custom_call" | custom-call | tf_op jit(solution)/shard_map/pallas_call | solution.py:513
Async XLA Ops:
  1.3 0.7 %copy-start = (f32[3,1,1,1,512]{4,3,2,1,0:T(1,128)S(1)}, f32[3,1,1,1,512]{4,3,2,1,0:T(1,128)}, u32[]{:S(2)}) copy-start(f32[3,1,1,1,512]{4,3,2,1,0:T(1,128)} %param.9) | copy-start | bytes 18436
  1.3 0.7 %copy-start.3 = (f32[1,1,1,512]{3,2,1,0:T(1,128)S(1)}, f32[1,1,1,512]{3,2,1,0:T(1,128)}, u32[]{:S(2)}) copy-start(f32[1,1,1,512]{3,2,1,0:T(1,128)} %param.11) | copy-start | bytes 6148
  1.3 0.7 %copy-start.4 = (f32[1,1,1,16]{3,2,1,0:T(1,128)S(1)}, f32[1,1,1,16]{3,2,1,0:T(1,128)}, u32[]{:S(2)}) copy-start(f32[1,1,1,16]{3,2,1,0:T(1,128)} %param.16) | copy-start | bytes 196
  27.7 0.6 %copy-start.1 = (f32[3,1,512]{2,1,0:T(1,128)}, f32[3,1,512]{2,1,0:T(1,128)S(1)}, u32[]{:S(2)}) copy-start(f32[3,1,512]{2,1,0:T(1,128)S(1)} %get-tuple-element.6.pos) | copy-start | bytes 18436
  28.3 0.6 %copy-start.2 = (f32[3,1,512]{2,1,0:T(1,128)}, f32[3,1,512]{2,1,0:T(1,128)S(1)}, u32[]{:S(2)}) copy-start(f32[3,1,512]{2,1,0:T(1,128)S(1)} %get-tuple-element.7.vel) | copy-start | bytes 18436

commit v8 on v6

--- a/solution.py
+++ b/solution.py
@@ -179,8 +179,8 @@
             copy.start()
             column_copies.append(copy)
 
-    def send_around(ref, rows, which):
-        for a, b, c in around:
+    def send_around(ref, rows, which, chosen):
+        for a, b, c in chosen:
             j = (a * 3 + b) * 3 + c
             pltpu.make_async_remote_copy(
                 src_ref=ref.at[pl.ds(home * ROWS, rows)],
@@ -195,13 +195,14 @@
         part = ref.at[pl.ds(0, rows)]
         pltpu.make_async_copy(part, part, sem).wait()
 
-    send_around(speeds, ROWS, 0)
+    send_around(speeds, ROWS, 0, [way for way in around if way[2] == 1])
     for load in loads[5:]:
         load.wait()
 
     lane_factor(z)
     for copy in column_copies:
         copy.wait_recv()
+    send_around(speeds, ROWS, 0, [way for way in around if way[2] != 1])
     for d in range(1, nz):
         lane_factor(lax.rem(z - d + nz, nz))
 
@@ -395,7 +396,7 @@
     pair_forces(table, forces)
     row = sum_row(block(forces, home), block(speeds, home))
     forces[pl.ds(home * ROWS + COORDS, 1), :] = row
-    send_around(forces, COORDS + 1, 2)
+    send_around(forces, COORDS + 1, 2, around)
     stage_start(row, 0, 0)
     old, new = sum_finish(0)
     for a, b, c in around + [(1, 1, 1)]:

time: 29.1 us -> 28.6 us (0.983)
  Pallas kernels: 25.7 us -> 25.2 us
    pallas_call x1, Pallas kernels: 25.7 us -> 25.2 us  [shards(): pl.pallas_call(functools.partial(cycle_kernel, mesh_shape), out_shape=[ja...]
where the time goes in v8:
time: 28.6 us; the launch traced here: 28.3 us
  Pallas kernels  25.2 us (88%)
  local copies, waits for them, and re-layouts  1.86 us (7%)
  between operations  1.31 us (5%)
    pallas_call x1, Pallas kernels, shards(): pl.pallas_call(functools.partial(cycle_kernel, mesh_shape), out_shape=[ja...  25.2 us
    unnamed x8, local copies, waits for them, and re-layouts  1.86 us

profile of v8, /device:TPU:0, one launch (start us, length us, event | category | flops | bytes accessed | tf_op | source)
XLA Modules:
  0.0 28.3 jit_solution(4082818409946638544)
XLA Ops:
  1.3 0.0 copy-start
  1.3 0.0 copy-start.1
  1.3 0.0 copy-start.2
  1.3 0.7 %copy-done = f32[3,1,1,1,512]{4,3,2,1,0:T(1,128)S(1)} copy-done((f32[3,1,1,1,512]{4,3,2,1,0:T(1,128)S(1)}, f32[3,1,1,1,512]{4,3,2,1,0:T(1,128)}, u32[]{:S(2)}) %copy-start) | copy-done | bytes 6168
  2.0 0.0 copy-done.1
  2.0 0.0 copy-done.2
  2.0 25.2 %shard_map.104 = (f32[3,1,512]{2,1,0:T(1,128)S(1)}, f32[3,1,512]{2,1,0:T(1,128)S(1)}) custom-call(f32[3,1,512]{2,1,0:T(1,128)S(1)} %bitcast.13, f32[3,1,512]{2,1,0:T(1,128)} %bitcast.21, f32[1,512]{1,0:T(1,128)S(1)} %bitcast.16, s32[32,512]{1,0:T(8,128)} %bitcast.18, s32[32,512]{1,0:T(8,128)} %bitcast.19, s32[1,1,1]{2,1,0:T(1,128)S(6)} %copy.15.count_in, ...), custom_call_target="tpu_custom_call" | custom-call | flops 10000000 | bytes 1000000 | tf_op jit(solution)/shard_map/pallas_call | solution.py:454
  27.2 0.6 %copy.16 = f32[3,1,1,1,512]{4,3,2,1,0:T(1,128)} copy(f32[3,1,1,1,512]{4,3,2,1,0:T(1,128)S(1)} %bitcast.15) | data formatting | bytes 12288
  27.8 0.6 %copy.17 = f32[3,1,1,1,512]{4,3,2,1,0:T(1,128)} copy(f32[3,1,1,1,512]{4,3,2,1,0:T(1,128)S(1)} %bitcast.14) | data formatting | bytes 12288
Async XLA Ops:
  1.3 0.7 %copy-start = (f32[3,1,1,1,512]{4,3,2,1,0:T(1,128)S(1)}, f32[3,1,1,1,512]{4,3,2,1,0:T(1,128)}, u32[]{:S(2)}) copy-start(f32[3,1,1,1,512]{4,3,2,1,0:T(1,128)} %param.9) | copy-start | bytes 18436
  1.3 0.7 %copy-start.1 = (f32[1,1,1,512]{3,2,1,0:T(1,128)S(1)}, f32[1,1,1,512]{3,2,1,0:T(1,128)}, u32[]{:S(2)}) copy-start(f32[1,1,1,512]{3,2,1,0:T(1,128)} %param.11) | copy-start | bytes 6148
  1.3 0.7 %copy-start.2 = (f32[1,1,1,16]{3,2,1,0:T(1,128)S(1)}, f32[1,1,1,16]{3,2,1,0:T(1,128)}, u32[]{:S(2)}) copy-start(f32[1,1,1,16]{3,2,1,0:T(1,128)} %param.16) | copy-start | bytes 196
